TPU v7x, 256 devices: a whole 4x4x8 slice. The times are simulated.
256 devices in a mesh: bl: 8 (over z_lo, y), row: 32 (over z_hi, x, core).
Axes of the slice: x: 4, y: 4, z: 8 (z_hi: 4, z_lo: 2; z = z_hi * 2 + z_lo), core: 2. Of those that a mesh axis runs over, the one named last changes fastest.
Arguments:
- visibilities: float32 [8, 32, 8, 2, 768], P('bl', 'row'), may hold values from -6 to 6
- kernels: float32 [8, 32, 8, 2, 8, 768], P('bl', 'row'), may hold values from 0.1 to 1
- offsets: int32 [8, 32, 8, 2, 768], P('bl', 'row'), may hold values from 0 to 120
- counts: int32 [8, 32, 8], P('bl', 'row'), may hold values from 0 to 768, as said below
- slot_tiles: int32 [8, 32, 8], P('bl', 'row'), may hold values from 0 to 127, as said below
- taper: float32 [8192, 8192], P(('row', 'bl')), may hold values from 0.5 to 1.5
Outputs:
- image: float32 [2, 8192, 8192], P(None, ('row', 'bl'))
Inputs may be any that keep to these rules, and one draw needn't show every extreme that they name: Slot s of a device holds its first counts visibilities; slot 0 of every device is full, and devices of the middle bands hold more. `slot_tiles`: tiles of a band are numbered tile row times 8192 / 128 plus tile column; the slots of one device name different tiles.
All inputs are finite; a program needn't handle non-finite values.
Results may differ from a plain program's by a relative error of at most 0.0001.
Values sent between devices are 32-bit elements; how exact they have to be, the bound alone decides.
No kernel may reach another device: no remote copies, remote signals or barrier semaphores. Data moves between devices by JAX's collectives and lax.ppermute only.
A program may use at most 128 MiB of HBM per device.

v0:
```python
import math

import jax
import jax.numpy as jnp
from jax import lax
from jax.sharding import PartitionSpec as P

TILE = 128
F1 = 64
F2 = 128


precise = lax.Precision.HIGHEST


def spread(kernel, offset_cells, side):
    cell_index = lax.iota(jnp.int32, side)
    spread_sum = jnp.zeros(offset_cells.shape + (side,), jnp.float32)
    for offset in range(kernel.shape[1]):
        matches = cell_index[None, None, :] == offset_cells[:, :, None] + offset
        spread_sum = spread_sum + kernel[:, offset, :, None] * matches.astype(jnp.float32)
    return spread_sum


def grid_tiles(visible, kernel, offset_cells, slot_counts):
    capacity = visible.shape[2]
    live_mask = (lax.iota(jnp.int32, capacity)[None, :] < slot_counts[:, None]).astype(jnp.float32)
    weights_row = spread(kernel[:, 0], offset_cells[:, 0], TILE) * live_mask[:, :, None]
    weights_col = spread(kernel[:, 1], offset_cells[:, 1], TILE)
    weighted = jnp.concatenate(
        [weights_row * visible[:, 0, :, None], weights_row * visible[:, 1, :, None]], axis=2
    )
    tile_grids = jnp.einsum("scu,scv->suv", weighted, weights_col, precision=precise)
    return tile_grids.reshape(visible.shape[0], 2, TILE, TILE)


def grid_blocks(visible, kernel, offset_cells, slot_counts):
    slot_count = visible.shape[0]
    block_size = math.gcd(slot_count, 4)
    turns = slot_count // block_size

    def one_block(pieces):
        return grid_tiles(pieces[0], pieces[1], pieces[2], pieces[3])

    blocked = (
        visible.reshape((turns, block_size) + visible.shape[1:]),
        kernel.reshape((turns, block_size) + kernel.shape[1:]),
        offset_cells.reshape((turns, block_size) + offset_cells.shape[1:]),
        slot_counts.reshape(turns, block_size),
    )
    result = lax.map(one_block, blocked)
    return result.reshape(slot_count, 2, TILE, TILE)


def dft_table(length, count_in, count_out):
    first_index = lax.iota(jnp.int32, count_in)[:, None]
    second_index = lax.iota(jnp.int32, count_out)[None, :]
    phase = first_index * second_index % length
    angle = phase.astype(jnp.float32) * (2.0 * math.pi / length)
    return (jnp.cos(angle), -jnp.sin(angle))


def complex_einsum(formula, left_pair, right_pair):
    left_re, left_im = left_pair
    right_re, right_im = right_pair
    real_part = jnp.einsum(formula, left_re, right_re, precision=precise) - jnp.einsum(
        formula, left_im, right_im, precision=precise
    )
    imag_part = jnp.einsum(formula, left_re, right_im, precision=precise) + jnp.einsum(
        formula, left_im, right_re, precision=precise
    )
    return (real_part, imag_part)


def column_transform(real_in, imag_in):
    row_total = real_in.shape[0]
    shaped = (real_in.reshape(row_total, F1, F2), imag_in.reshape(row_total, F1, F2))
    sectioned = complex_einsum("rab,ak->rkb", shaped, dft_table(F1, F1, F1))
    twist_re, twist_im = dft_table(F1 * F2, F1, F2)
    turned = (
        sectioned[0] * twist_re - sectioned[1] * twist_im,
        sectioned[0] * twist_im + sectioned[1] * twist_re,
    )
    result = complex_einsum("rkb,bq->rqk", turned, dft_table(F2, F2, F2))
    return (result[0].reshape(row_total, F1 * F2), result[1].reshape(row_total, F1 * F2))


def row_transform(shaped, formula, row_count, group_count, strip_rows):
    band_rows = group_count * strip_rows
    total_rows = row_count * band_rows
    sectioned = complex_einsum(
        formula + ",rk->kbic", shaped, dft_table(row_count, row_count, row_count)
    )
    twist_re, twist_im = dft_table(total_rows, row_count, band_rows)
    twist_re = twist_re.reshape(row_count, group_count, strip_rows)[..., None]
    twist_im = twist_im.reshape(row_count, group_count, strip_rows)[..., None]
    turned = (
        sectioned[0] * twist_re - sectioned[1] * twist_im,
        sectioned[0] * twist_im + sectioned[1] * twist_re,
    )
    second_re, second_im = dft_table(band_rows, band_rows, band_rows)
    second_pair = (
        second_re.reshape(group_count, strip_rows, band_rows),
        second_im.reshape(group_count, strip_rows, band_rows),
    )
    result = complex_einsum("kbic,biq->cqk", turned, second_pair)
    column_count = result[0].shape[0]
    scale = 1.0 / total_rows
    return (
        result[0].reshape(column_count, total_rows) * scale,
        result[1].reshape(column_count, total_rows) * scale,
    )


def body(visibilities, kernels, offsets, counts, slot_tiles, taper):
    group_count = lax.axis_size("bl")
    row_count = lax.axis_size("row")
    strip_rows = taper.shape[0]
    grid_side = taper.shape[1]
    band_rows = strip_rows * group_count
    tile_columns = grid_side // TILE
    tile_grids = grid_blocks(visibilities[0, 0], kernels[0, 0], offsets[0, 0], counts[0, 0])
    slot_count = tile_grids.shape[0]
    tile_numbers = slot_tiles[0, 0]

    def place_slot(slot_index, partial_value):
        tile_number = tile_numbers[slot_index]
        first_row = tile_number // tile_columns * TILE
        first_col = tile_number % tile_columns * TILE
        corner = (jnp.int32(0), first_row, first_col)
        current = lax.dynamic_slice(partial_value, corner, (2, TILE, TILE))
        return lax.dynamic_update_slice(partial_value, current + tile_grids[slot_index], corner)

    band_grid = lax.fori_loop(
        0, slot_count, place_slot, jnp.zeros((2, band_rows, grid_side), jnp.float32)
    )
    summed = lax.psum_scatter(band_grid, "bl", scatter_dimension=1, tiled=True)
    tapered = summed * taper[None]
    freq_re, freq_im = column_transform(tapered[0], tapered[1])
    column_share = grid_side // (row_count * group_count)
    stacked = jnp.stack([freq_re, freq_im]).reshape(
        2, strip_rows, row_count, group_count, column_share
    )
    moved = lax.all_to_all(
        lax.all_to_all(stacked, "row", split_axis=2, concat_axis=1, tiled=True),
        "bl",
        split_axis=3,
        concat_axis=1,
        tiled=True,
    )
    arranged = moved.reshape(2, group_count, row_count, strip_rows, column_share)
    formula = "bric"
    image_re, image_im = row_transform(
        (arranged[0], arranged[1]), formula, row_count, group_count, strip_rows
    )
    return jnp.stack([image_re, image_im])


def solution(mesh):
    in_specs = (
        P("bl", "row", None, None, None),
        P("bl", "row", None, None, None, None),
        P("bl", "row", None, None, None),
        P("bl", "row", None),
        P("bl", "row", None),
        P(("row", "bl"), None),
    )
    out_specs = P(None, ("row", "bl"), None)
    return jax.shard_map(body, mesh=mesh, in_specs=in_specs, out_specs=out_specs, check_vma=False)
```

profile of v0, /device:TPU:1, one launch (start us, length us, event | category | flops | bytes accessed | tf_op | source)
XLA Modules:
  0.0 534.2 jit_solution(10014762911124144232)
XLA Ops:
  7.1 1.3 reduce.3
  8.5 18.8 %while.25 = (s32[]{:T(128)}, f32[2,4,2,128,128]{4,3,2,1,0:T(8,128)S(1)}, s32[2,4,2,768]{3,2,1,0:T(2,128)}, f32[2,4,2,8,768]{4,3,2,1,0:T(8,128)}, s32[2,4]{1,0:T(2,128)S(1)}, /*index=5*/f32[2,4,2,768]{3,2,1,0:T(2,128)}, s32[]{:T(128)}) while((s32[]{:T(128)}, f32[2,4,2,128,128]{4,3,2,1,0:T(8,128)S(1)}, s32[2,4,2,768]{3,2,1,0:T(2,128)}, ...), condition=%wide.region_1.2_spmd, body=%wide.region_0.1_spmd.sunk | while | flops 1228062720 | bytes 10371217 | solution.py:51
  8.5 0.9 constant_dynamic-slice_fusion.8
  9.6 0.7 constant_dynamic-slice_fusion.9
  10.4 0.7 constant_dynamic-slice_fusion.7
  11.3 2.0 broadcast_multiply_fusion.4
  13.3 4.5 fusion.220
  17.9 0.9 constant_dynamic-slice_fusion.8
  20.7 2.0 broadcast_multiply_fusion.4
  22.7 4.5 fusion.220
  27.3 7.8 %broadcast_in_dim.7 = f32[2,256,8192]{2,1,0:T(8,128)} broadcast(f32[]{:T(128)} %constant.249.clone.1), dimensions={} | broadcast | bytes 16777220 | tf_op jit(solution)/shard_map/broadcast_in_dim | solution.py:135
  35.1 38.4 %while.26 = (s32[]{:T(128)}, f32[2,256,8192]{2,1,0:T(8,128)}, s32[8]{0:T(128)S(1)}, f32[8,2,128,128]{3,2,1,0:T(8,128)S(1)}, s32[]{:T(128)}, /*index=5*/s32[]{:T(...) while((s32[]{:T(128)}, f32[2,256,8192]{2,1,0:T(8,128)}, ...), condition=%wide.region_3.4_spmd, body=%wide.region_2.3_spmd.sunk | while | flops 32797 | bytes 394152 | solution.py:134
  38.3 1.6 fusion.221
  43.1 1.6 fusion.221
  47.8 1.6 fusion.221
  52.6 1.6 fusion.221
  57.4 1.6 fusion.221
  62.2 1.6 fusion.221
  66.9 1.6 fusion.221
  71.7 1.6 fusion.221
  73.7 177.8 %reduce-scatter.2.cloned.1.call-done = f32[2,32,8192]{2,1,0:T(8,128)} async-done(((f32[2,256,8192]{2,1,0:T(8,128)}), f32[2,32,8192]{2,1,0:T(8,128)}) %reduce-scatter.2.cloned.1.call-update) | async-done | bytes 2097168 | tf_op jit(solution)/shard_map/reduce_scatter | solution.py:137
  251.5 1.8 broadcast_multiply_fusion.2
  253.6 1.2 fusion.97
  254.8 1.2 fusion.93
  256.1 1.2 convolution_subtract_fusion.2
  257.3 1.2 convolution_add_fusion.2
  258.4 1.2 fusion.53
  259.7 1.2 fusion.51
  260.9 2.2 fusion.42
  263.1 3.2 copy.33
  266.3 4.3 stack.12
  270.6 2.2 fusion.41
  272.8 1.8 copy.34
  274.7 2.5 stack.13
  277.2 6.0 %copy_bitcast_fusion.3 = f32[32,2,32,8,32]{4,3,2,1,0:T(8,128)} fusion(f32[1,32,32,8,32]{4,3,2,1,0:T(8,128)} %stack.13, f32[1,32,32,8,32]{4,3,2,1,0:T(8,128)} %stack.12), kind=kLoop, calls=%fused_computation.292 | loop fusion | flops 524288 | bytes 4194304
  283.2 6.8 %reshape.309 = f32[32,1,16384]{2,1,0:T(1,128)S(1)} reshape(f32[32,2,32,8,32]{4,3,2,1,0:T(8,128)} %copy_bitcast_fusion.3) | data formatting | bytes 4194304
  290.0 51.7 %all_to_all.33 = f32[32,1,16384]{2,1,0:T(1,128)} all-to-all(f32[32,1,16384]{2,1,0:T(1,128)S(1)} %reshape.309), channel_id=1, replica_groups=mesh['bl'=8,'row'=32] {'row'}, dimensions={0} | all-to-all | bytes 4194304 | tf_op jit(solution)/shard_map/all_to_all | solution.py:145
  342.1 7.4 %reduce.4 = f32[32,16384]{1,0:T(8,128)S(1)} reduce(f32[32,1,16384]{2,1,0:T(1,128)} %all_to_all.33, f32[]{:T(128)} %broadcast.434), dimensions={1}, to_apply=%all_to_all.24.reduce_sub_computation | reduce | bytes 4194308 | tf_op jit(solution)/shard_map/all_to_all | solution.py:145
  349.5 4.8 reshape.310
  354.3 7.6 %bitcast_bitcast_fusion = f32[2,32,32,1,8,32]{5,4,2,0,1,3:T(8,128)} fusion(f32[32,2,32,8,32]{4,3,2,1,0:T(8,128)} %reshape.310), kind=kLoop, calls=%fused_computation.291 | loop fusion | bytes 4194304 | tf_op jit(solution)/shard_map/all_to_all | solution.py:145
  361.9 10.2 %copy.55 = f32[2,32,32,1,8,32]{2,1,5,0,4,3:T(8,128)} copy(f32[2,32,32,1,8,32]{5,4,2,0,1,3:T(8,128)} %bitcast_bitcast_fusion) | data formatting | bytes 4194304 | tf_op jit(solution)/shard_map/all_to_all | solution.py:145
  372.1 7.7 %reshape.299 = f32[2,1024,1,8,32]{1,4,0,2,3:T(8,128)} reshape(f32[2,32,32,1,8,32]{2,1,5,0,4,3:T(8,128)} %copy.55) | data formatting | bytes 4194304 | tf_op jit(solution)/shard_map/all_to_all | solution.py:145
  379.8 12.3 %all-to-all-start.1 = ((f32[2,1024,1,8,32]{1,4,0,2,3:T(8,128)}), f32[2,1024,1,8,32]{1,4,0,2,3:T(8,128)S(1)}, u32[]{:S(2)}, u32[]{:S(2)}) async-start(f32[2,1024,1,8,32]{1,4,0,2,3:T(8,128)} %reshape.299), calls=%async_computation.2 | async-start | bytes 4194304 | tf_op jit(solution)/shard_map/all_to_all | solution.py:144
  392.7 25.5 %all-to-all-done.1 = f32[2,1024,1,8,32]{1,4,0,2,3:T(8,128)S(1)} async-done(((f32[2,1024,1,8,32]{1,4,0,2,3:T(8,128)}), f32[2,1024,1,8,32]{1,4,0,2,3:T(8,128)S(1)}, u32[]{:S(2)}, u32[]{:S(2)}) %all-to-all-start.1) | async-done | bytes 2097184 | tf_op jit(solution)/shard_map/all_to_all | solution.py:144
  418.2 1.2 fusion.197
  419.4 3.9 squeeze.43
  423.3 6.9 %copy.38 = f32[8,32,32,32]{3,1,2,0:T(8,128)} copy(f32[8,32,32,32]{2,1,3,0:T(8,128)} %squeeze.43) | data formatting | bytes 2097152 | tf_op jit(solution)/shard_map/squeeze | solution.py:154
  430.2 8.0 %fusion.114 = f32[32,8,32,32]{3,0,2,1:T(8,128)} fusion(f32[8,32,32,32]{3,1,2,0:T(8,128)} %copy.38), kind=kOutput, calls=%fused_computation.213 | convolution fusion | flops 100677632 | bytes 2097152 | tf_op jit(solution)/shard_map/bric,rk->kbic/dot_general | solution.py:66
  438.2 5.2 fusion.116
  443.4 2.7 squeeze.80
  446.1 7.1 %copy.39 = f32[8,32,32,32]{3,1,2,0:T(8,128)} copy(f32[8,32,32,32]{2,1,3,0:T(8,128)} %squeeze.80) | data formatting | bytes 2097152 | tf_op jit(solution)/shard_map/squeeze | solution.py:154
  453.2 7.7 %convolution_subtract_fusion = f32[32,8,32,32]{3,0,2,1:T(8,128)S(1)} fusion(f32[32,8,32,32]{3,0,2,1:T(8,128)} %fusion.114, f32[8,32,32,32]{3,1,2,0:T(8,128)} %copy.39), kind=kOutput, calls=%fused_computation.110 | convolution fusion | flops 100940800 | bytes 3145728 | tf_op jit(solution)/shard_map/bric,rk->kbic/dot_general | solution.py:66
  460.9 7.5 %multiply_subtract_fusion = (f32[32,8,32,32]{3,0,2,1:T(8,128)}, f32[32,8,32,32]{3,0,2,1:T(8,128)}) fusion(f32[32,8,32,32]{3,0,2,1:T(8,128)S(1)} %convolution_subtract_fusion, f32[32,8,32]{0,2,1:T(8,128)S(1)} %get-tuple-element.237, f32[32,8,32]{0,2,1:T(8,128)S(1)} %get-tuple-element.236, f32[32,8,32,32]{3,0,2,1:T(8,128)S(1)} %copy-done.3, ...), kind=kOutput, calls=%fused_computation.108 | convolution fusion | flops 102512640 | bytes 5308416 | tf_op jit(solution)/shard_map/bric,rk->kbic/dot_general | solution.py:69
  468.4 6.1 %copy.43 = f32[32,8,32,32]{2,3,1,0:T(8,128)} copy(f32[32,8,32,32]{3,0,2,1:T(8,128)} %get-tuple-element.231) | data formatting | bytes 2097152 | tf_op jit(solution)/shard_map/add | solution.py:99
  474.5 9.0 %convolution_bitcast_fusion.2 = f32[256,32,32]{0,2,1:T(8,128)S(1)} fusion(f32[32,8,32,32]{2,3,1,0:T(8,128)} %copy.43, s32[8,32]{1,0:T(8,128)S(1)} %multiply_add_fusion.4), kind=kOutput, calls=%fused_computation.114 | convolution fusion | flops 806289408 | bytes 2098176 | tf_op jit(solution)/shard_map/kbic,biq->cqk/dot_general | solution.py:66
  483.5 6.0 %convolution_bitcast_fusion = f32[256,32,32]{0,2,1:T(8,128)S(1)} fusion(f32[32,8,32,32]{2,3,1,0:T(8,128)S(1)} %copy-done.2, s32[8,32]{1,0:T(8,128)S(1)} %multiply_add_fusion.4), kind=kOutput, calls=%fused_computation.112 | convolution fusion | flops 806223872 | bytes 2098176 | tf_op jit(solution)/shard_map/kbic,biq->cqk/dot_general | solution.py:69
  489.5 6.0 %copy.42 = f32[32,8,32,32]{2,3,1,0:T(8,128)} copy(f32[32,8,32,32]{3,0,2,1:T(8,128)} %get-tuple-element.230) | data formatting | bytes 2097152 | tf_op jit(solution)/shard_map/sub | solution.py:98
  495.5 8.7 %fusion.45 = f32[32,256,32]{1,0,2:T(8,128)S(1)} fusion(f32[256,32,32]{0,2,1:T(8,128)S(1)} %convolution_bitcast_fusion.2, f32[32,8,32,32]{2,3,1,0:T(8,128)} %copy.42, s32[8,32]{1,0:T(8,128)S(1)} %multiply_add_fusion.4), kind=kOutput, calls=%fused_computation.124 | convolution fusion | flops 806748160 | bytes 3146752 | tf_op jit(solution)/shard_map/kbic,biq->cqk/dot_general | solution.py:66
  504.2 2.7 copy.44
  506.9 3.5 mul.689
  510.4 9.0 %fusion.48 = f32[32,256,32]{1,0,2:T(8,128)S(1)} fusion(f32[256,32,32]{0,2,1:T(8,128)S(1)} %convolution_bitcast_fusion, f32[32,8,32,32]{2,3,1,0:T(8,128)} %copy.42, s32[8,32]{1,0:T(8,128)S(1)} %multiply_add_fusion.4), kind=kOutput, calls=%fused_computation.127 | convolution fusion | flops 806813696 | bytes 3146752 | tf_op jit(solution)/shard_map/kbic,biq->cqk/dot_general | solution.py:69
  519.4 2.7 copy.47
  522.1 3.5 mul.692
  525.6 1.5 pad_maximum_fusion.1
  (56 shorter events, 9.4 us)
Async XLA Ops:
  6.5 244.9 %reduce-scatter.2.cloned.1.call-start = ((), (), s32[]{:S(2)}) async-start(), calls=%async_computation.3 | async-start | bytes 18874368 | tf_op jit(solution)/shard_map/reduce_scatter | solution.py:137
  27.3 7.8 %copy-start.5 = (s32[1,1,8]{2,1,0:T(1,128)S(1)}, s32[1,1,8]{2,1,0:T(1,128)}, u32[]{:S(2)}) copy-start(s32[1,1,8]{2,1,0:T(1,128)} %param.14) | copy-start | bytes 100
  73.5 178.0 %copy-start.4 = (f32[32,8192]{1,0:T(8,128)S(1)}, f32[32,8192]{1,0:T(8,128)}, u32[]{:S(2)}) copy-start(f32[32,8192]{1,0:T(8,128)} %param.15) | copy-start | bytes 3145732
  379.8 38.4 %all-to-all-start.1 = ((f32[2,1024,1,8,32]{1,4,0,2,3:T(8,128)}), f32[2,1024,1,8,32]{1,4,0,2,3:T(8,128)S(1)}, u32[]{:S(2)}, u32[]{:S(2)}) async-start(f32[2,1024,1,8,32]{1,4,0,2,3:T(8,128)} %reshape.299), calls=%async_computation.2 | async-start | bytes 4194304 | tf_op jit(solution)/shard_map/all_to_all | solution.py:144
  430.2 8.0 %copy-start.1 = (f32[8,32,32,32]{3,1,2,0:T(8,128)S(1)}, f32[8,32,32,32]{3,1,2,0:T(8,128)}, u32[]{:S(2)}) copy-start(f32[8,32,32,32]{3,1,2,0:T(8,128)} %copy.38) | copy-start | bytes 3145732
  453.2 7.7 %copy-start = (f32[8,32,32,32]{3,1,2,0:T(8,128)S(1)}, f32[8,32,32,32]{3,1,2,0:T(8,128)}, u32[]{:S(2)}) copy-start(f32[8,32,32,32]{3,1,2,0:T(8,128)} %copy.39) | copy-start | bytes 3145732
  453.2 7.7 %copy-start.3 = (f32[32,8,32,32]{3,0,2,1:T(8,128)S(1)}, f32[32,8,32,32]{3,0,2,1:T(8,128)}, u32[]{:S(2)}) copy-start(f32[32,8,32,32]{3,0,2,1:T(8,128)} %fusion.116) | copy-start | bytes 3145732
  474.5 9.1 %copy-start.2 = (f32[32,8,32,32]{2,3,1,0:T(8,128)S(1)}, f32[32,8,32,32]{2,3,1,0:T(8,128)}, u32[]{:S(2)}) copy-start(f32[32,8,32,32]{2,3,1,0:T(8,128)} %copy.43) | copy-start | bytes 3145732
Sparse Core Ops, SparseCore 0:
  73.7 177.7 reduce-scatter.1
where the time goes:
time: 542 us; the launch traced here: 534 us
  waiting for transfers between devices  203 us (37%)
  local copies, waits for them, and re-layouts  115 us (21%)
  matrix products  81.7 us (15%)
  blocking collectives  51.7 us (10%)
  other arithmetic  35.7 us (7%)
  loops' own time  20.9 us (4%)
  between operations  13.9 us (3%)
  starting transfers between devices  12.3 us (2%)
    reduce_scatter x1, waiting for transfers between devices, body(): summed = lax.psum_scatter(band_grid, 'bl', scatter_dimension=1, tiled=True)  178 us
    all_to_all x1, blocking collectives, body(): lax.all_to_all(stacked, 'row', split_axis=2, concat_axis=1, tiled=True)  51.7 us
    all_to_all x4, local copies, waits for them, and re-layouts, body(): lax.all_to_all(stacked, 'row', split_axis=2, concat_axis=1, tiled=True)  26 us
    all_to_all x1, waiting for transfers between devices, body(): lax.all_to_all(lax.all_to_all(stacked, 'row', split_axis=2, concat_axis=1...  25.5 us
    another operation x1, loops' own time, body(): lax.fori_loop(0, slot_count, place_slot, jnp.zeros((2, band_rows, grid_si...  20.7 us
    dot_general x4, matrix products, complex_einsum(): jnp.einsum(formula, left_im, right_im, precision=precise)  20.1 us
    dot_general x4, matrix products, complex_einsum(): jnp.einsum(formula, left_re, right_re, precision=precise)  19.1 us
    dot_general x4, matrix products, complex_einsum(): jnp.einsum(formula, left_im, right_re, precision=precise)  16.9 us
  transfers between devices with their start and end apart: 2, of which 2 were waited for; matrix products, arithmetic and copies ran while one was open for 0% of the time, Pallas kernels for 0%

commit v1 on v0

v1 whole, which is shorter than its diff:
```python
import math

import jax
import jax.numpy as jnp
import ml_dtypes
import numpy as np
from jax import lax
from jax.experimental import pallas as pl
from jax.experimental.pallas import tpu as pltpu
from jax.sharding import PartitionSpec as P

G = 8192
TILE = 128
SUP = 8
SLOTS = 8
CAP = 768
N_BL = 8
N_ROW = 32
BANDS = 2
STRIP = TILE // N_BL
COLS = G // TILE
F32 = jnp.float32
BF16 = jnp.bfloat16
NT = (((1,), (1,)), ((), ()))


def unit(length, phase):
    angle = 2.0 * np.pi * (np.asarray(phase, np.int64) % length) / length
    return np.cos(angle), np.sin(angle)


def real_form(cosine, sine):
    return np.block([[cosine, sine], [-sine, cosine]])


def halves(table):
    high = table.astype(ml_dtypes.bfloat16)
    low = (table - high.astype(np.float64)).astype(ml_dtypes.bfloat16)
    return high, low


def split(value):
    high = value.astype(BF16)
    low = (value - high.astype(F32)).astype(BF16)
    return high, low


def add(left, right):
    return (left[0] + right[0], left[1] + right[1])


def sub(left, right):
    return (left[0] - right[0], left[1] - right[1])


def dft4(a, b, c, d):
    s, t = add(a, c), sub(a, c)
    u, v = add(b, d), sub(b, d)
    w = (v[1], -v[0])
    return [add(s, u), add(t, w), sub(s, u), sub(t, w)]


def dft8(x):
    even = dft4(x[0], x[2], x[4], x[6])
    odd = dft4(x[1], x[3], x[5], x[7])
    r = math.sqrt(0.5)
    turned = [
        odd[0],
        ((odd[1][0] + odd[1][1]) * r, (odd[1][1] - odd[1][0]) * r),
        (odd[2][1], -odd[2][0]),
        ((odd[3][1] - odd[3][0]) * r, (odd[3][1] + odd[3][0]) * -r),
    ]
    return [add(e, o) for e, o in zip(even, turned)] + [sub(e, o) for e, o in zip(even, turned)]


def mul(x, cosine, sine):
    return (x[0] * cosine + x[1] * sine, x[1] * cosine - x[0] * sine)


def grid_kernel(counts, tiles, vis, taps, offs, out):
    sub_index = lax.broadcasted_iota(jnp.int32, (SUP, CAP), 0)
    lane = lax.broadcasted_iota(jnp.int32, (1, CAP), 1)

    def place(block, taken):
        pieces = [jnp.where(taken == x, block, 0.0) for x in range(TILE // SUP)]
        return jnp.concatenate(pieces, axis=0).astype(BF16)

    def rotated(s, axis):
        first = jnp.broadcast_to(offs[s, axis : axis + 1, :], (SUP, CAP))
        shift = first & (SUP - 1)
        value = taps[s, axis]
        for bit in (1, 2, 4):
            value = jnp.where((shift & bit) != 0, pltpu.roll(value, bit, 0), value)
        taken = (first >> 3) + jnp.where(sub_index < shift, 1, 0)
        return value, taken

    def one_slot(s, carry):
        live = lane < counts[s]
        value, taken = rotated(s, 0)
        lefts = [split(value * jnp.where(live, vis[s, p : p + 1, :], 0.0)) for p in range(2)]
        left = jnp.concatenate(
            [place(lefts[p][h].astype(F32), taken) for h in range(2) for p in range(2)], axis=0
        )
        value, taken = rotated(s, 1)
        rights = split(value)
        right = jnp.concatenate([place(rights[h].astype(F32), taken) for h in range(2)], axis=0)
        prod = lax.dot_general(left, right, NT, preferred_element_type=F32)
        tile = (prod[:256, :128] + prod[256:, :128]) + (prod[:256, 128:] + prod[256:, 128:])
        for p in range(2):
            for d in range(N_BL):
                start = p * TILE + d * STRIP
                out[d, pl.ds(s * 32 + p * STRIP, STRIP), :] = tile[start : start + STRIP]
        number = jnp.full((1, TILE), tiles[s], jnp.int32).astype(F32)
        for d in range(N_BL):
            out[d, pl.ds(256 + s, 1), :] = number
        return carry

    lax.fori_loop(0, SLOTS, one_slot, 0)


def grid_call(counts, tiles, vis, taps, offs):
    smem = pl.BlockSpec(memory_space=pltpu.SMEM)
    vmem = pl.BlockSpec(memory_space=pltpu.VMEM)
    return pl.pallas_call(
        grid_kernel,
        out_shape=jax.ShapeDtypeStruct((N_BL, 264, TILE), F32),
        in_specs=[smem, smem, vmem, vmem, vmem],
        out_specs=vmem,
        compiler_params=pltpu.CompilerParams(vmem_limit_bytes=40 << 20),
    )(counts, tiles, vis, taps, offs)


def column_kernel(
    parity, strips, taper_a, taper_b, tw, wh, wl, out,
    taper, cells, half, xh, xl, ob, number, place, sem_in, sem_out,
):
    par = parity[0]
    in_a = pltpu.make_async_copy(taper_a, taper.at[par], sem_in.at[0])
    in_b = pltpu.make_async_copy(taper_b, taper.at[1 - par], sem_in.at[1])
    in_a.start()
    in_b.start()
    number[...] = strips[:, 256:264, :].reshape(64, TILE).astype(jnp.int32)
    to_scalar = pltpu.make_async_copy(number, place, sem_in.at[2])
    to_scalar.start()
    cells[...] = jnp.zeros_like(cells)
    to_scalar.wait()

    def add_strip(step, carry):
        tile = place[step, 0]
        start = pl.multiple_of((step % SLOTS) * 32, 32)
        rows = strips[step // SLOTS, pl.ds(start, 32), :]
        cells[tile] = cells[tile] + rows
        return carry

    lax.fori_loop(0, 64, add_strip, 0, unroll=4)
    in_a.wait()
    in_b.wait()
    copies = []
    for tr in range(BANDS):
        for a0 in range(8):
            x = []
            for a1 in range(8):
                a = a1 * 8 + a0
                t = taper[tr, :, a * TILE : (a + 1) * TILE]
                x.append((cells[tr * COLS + a, 0:16] * t, cells[tr * COLS + a, 16:32] * t))
            for k0, y in enumerate(dft8(x)):
                if a0 * k0:
                    c, s = unit(64, a0 * k0)
                    y = mul(y, float(c), float(s))
                half[k0 * 8 + a0, 0:16] = y[0]
                half[k0 * 8 + a0, 16:32] = y[1]
        for k0 in range(8):
            x = [(half[k0 * 8 + a0, 0:16], half[k0 * 8 + a0, 16:32]) for a0 in range(8)]
            for k1, y in enumerate(dft8(x)):
                k = k0 + 8 * k1
                y = mul(y, tw[0, k : k + 1, :], tw[1, k : k + 1, :])
                for p in range(2):
                    high, low = split(y[p])
                    xh[tr, k * 16 : k * 16 + 16, p * TILE : (p + 1) * TILE] = high
                    xl[tr, k * 16 : k * 16 + 16, p * TILE : (p + 1) * TILE] = low
        for block in range(4):
            rows_h = xh[tr, block * 256 : (block + 1) * 256, :]
            rows_l = xl[tr, block * 256 : (block + 1) * 256, :]
            prod = lax.dot_general(wh[...], rows_h, NT, preferred_element_type=F32)
            prod += lax.dot_general(wl[...], rows_h, NT, preferred_element_type=F32)
            prod += lax.dot_general(wh[...], rows_l, NT, preferred_element_type=F32)
            kh = block // 2
            for p in range(2):
                for m in range(2):
                    row = (p * 2 + tr) * 4 + (block % 2) * 2 + m
                    ob[kh * 16 + row] = prod[p * TILE : (p + 1) * TILE, m * TILE : (m + 1) * TILE]
                    copy = pltpu.make_async_copy(
                        ob.at[kh * 16 + row], out.at[:, kh, row, :], sem_out.at[kh * 16 + row]
                    )
                    copy.start()
                    copies.append(copy)
    for copy in copies:
        copy.wait()


def column_tables():
    k = np.arange(COLS)[:, None]
    y = np.arange(TILE)[None, :]
    turn = np.stack(unit(G, k * y)).astype(np.float32)
    q = np.arange(TILE)[:, None]
    high, low = halves(real_form(*unit(TILE, q * y)))
    return turn, high, low


def column_call(parity, strips, taper_a, taper_b):
    smem = pl.BlockSpec(memory_space=pltpu.SMEM)
    vmem = pl.BlockSpec(memory_space=pltpu.VMEM)
    hbm = pl.BlockSpec(memory_space=pl.ANY)
    return pl.pallas_call(
        column_kernel,
        out_shape=jax.ShapeDtypeStruct((TILE, 2, 16, TILE), F32),
        in_specs=[smem, vmem, hbm, hbm, vmem, vmem, vmem],
        out_specs=hbm,
        scratch_shapes=[
            pltpu.VMEM((2, STRIP, G), F32),
            pltpu.VMEM((BANDS * COLS, 32, TILE), F32),
            pltpu.VMEM((64, 32, TILE), F32),
            pltpu.VMEM((BANDS, 1024, 256), BF16),
            pltpu.VMEM((BANDS, 1024, 256), BF16),
            pltpu.VMEM((32, TILE, TILE), F32),
            pltpu.VMEM((64, TILE), jnp.int32),
            pltpu.SMEM((64, TILE), jnp.int32),
            pltpu.SemaphoreType.DMA((3,)),
            pltpu.SemaphoreType.DMA((32,)),
        ],
        compiler_params=pltpu.CompilerParams(vmem_limit_bytes=40 << 20),
    )(parity, strips, taper_a, taper_b, *column_tables())


def row_kernel(arrived, w1h, w1l, tw, gh, gl, out, x, at, bh, bl, sem):
    copies = []
    for dl in range(4):
        for s in range(16):
            pt, mb = s // 4, s % 4
            copy = pltpu.make_async_copy(
                arrived.at[:, dl, s, :],
                x.at[dl, pl.ds(pt * 64, 64), pl.ds(mb * TILE, TILE)],
                sem.at[dl * 16 + s],
            )
            copy.start()
            copies.append(copy)
    for dl in range(4):
        for copy in copies[dl * 16 : dl * 16 + 16]:
            copy.wait()
        high, low = split(x[dl])
        prod = jnp.dot(w1h[...], high, preferred_element_type=F32)
        prod += jnp.dot(w1l[...], high, preferred_element_type=F32)
        prod += jnp.dot(w1h[...], low, preferred_element_type=F32)
        at[dl] = prod

    def radix(step, carry):
        mb, block = step // 8, step % 8
        rows = pl.ds(pl.multiple_of(block * 16, 16), 16)
        rows_im = pl.ds(pl.multiple_of(TILE + block * 16, 16), 16)
        lanes = pl.ds(pl.multiple_of(mb * TILE, TILE), TILE)
        parts = [
            mul((at[dl, rows, lanes], at[dl, rows_im, lanes]), tw[dl, 0, rows, :], tw[dl, 1, rows, :])
            for dl in range(4)
        ]
        to_rows = pl.ds(pl.multiple_of(mb * TILE + block * 16, 16), 16)
        for kb, y in enumerate(dft4(*parts)):
            for p in range(2):
                high, low = split(y[p])
                bh[kb, to_rows, p * TILE : (p + 1) * TILE] = high
                bl[kb, to_rows, p * TILE : (p + 1) * TILE] = low
        return carry

    lax.fori_loop(0, 32, radix, 0)
    for kb in range(4):
        prod = lax.dot_general(gh[kb], bh[kb], NT, preferred_element_type=F32)
        prod += lax.dot_general(gl[kb], bh[kb], NT, preferred_element_type=F32)
        prod += lax.dot_general(gh[kb], bl[kb], NT, preferred_element_type=F32)
        for p in range(2):
            for k2 in range(16):
                row = p * TILE + k2 * 8
                to = (k2 * 4 + kb) * TILE
                for mb in range(4):
                    out[p, mb * 8 : mb * 8 + 8, to : to + TILE] = prod[
                        row : row + 8, mb * TILE : (mb + 1) * TILE
                    ]


def row_tables():
    ka = np.arange(TILE)[:, None]
    tr, r, dh = np.meshgrid(np.arange(2), np.arange(N_ROW), np.arange(2), indexing="ij")
    coarse = (r * 4 + tr * 2 + dh).reshape(1, TILE)
    w1h, w1l = halves(real_form(*unit(TILE, ka * coarse)))
    fine = np.arange(TILE)[None, :] % 16
    turn = np.stack([np.stack(unit(G, ka * (dl * 16 + fine))) for dl in range(4)])
    k2, j = np.meshgrid(np.arange(16), np.arange(8), indexing="ij")
    k2, j = k2.reshape(TILE, 1), j.reshape(TILE, 1)
    jj, i = np.meshgrid(np.arange(8), np.arange(16), indexing="ij")
    jj, i = jj.reshape(1, TILE), i.reshape(1, TILE)
    same = (j == jj) / G
    last = []
    for kb in range(4):
        cosine, sine = unit(64, i * (kb + 4 * k2))
        last.append(real_form(cosine * same, sine * same))
    gh, gl = halves(np.stack(last))
    return w1h, w1l, turn.astype(np.float32), gh, gl


def row_call(arrived):
    vmem = pl.BlockSpec(memory_space=pltpu.VMEM)
    hbm = pl.BlockSpec(memory_space=pl.ANY)
    return pl.pallas_call(
        row_kernel,
        out_shape=jax.ShapeDtypeStruct((2, 32, G), F32),
        in_specs=[hbm, vmem, vmem, vmem, vmem, vmem],
        out_specs=vmem,
        scratch_shapes=[
            pltpu.VMEM((4, 256, 512), F32),
            pltpu.VMEM((4, 256, 512), F32),
            pltpu.VMEM((4, 512, 256), BF16),
            pltpu.VMEM((4, 512, 256), BF16),
            pltpu.SemaphoreType.DMA((64,)),
        ],
        compiler_params=pltpu.CompilerParams(vmem_limit_bytes=40 << 20),
    )(arrived, *row_tables())


def body(visibilities, kernels, offsets, counts, slot_tiles, taper):
    me = lax.axis_index("bl")
    low = me < N_BL // 2
    first = jnp.where(low, 0, STRIP)
    taper_a = lax.dynamic_slice(taper, (first, 0), (STRIP, G))
    taper_b = lax.dynamic_slice(taper, (STRIP - first, 0), (STRIP, G))
    to_a = [(s, (2 * s + (s >= 4)) % 8) for s in range(N_BL)]
    to_b = [(s, (2 * s + (s < 4)) % 8) for s in range(N_BL)]
    taper_a = lax.ppermute(taper_a, "bl", to_a)
    taper_b = lax.ppermute(taper_b, "bl", to_b)
    strips = grid_call(
        counts[0, 0], slot_tiles[0, 0], visibilities[0, 0], kernels[0, 0], offsets[0, 0]
    )
    strips = lax.all_to_all(strips, "bl", 0, 0, tiled=True)
    parity = (me % 2).reshape(1).astype(jnp.int32)
    leaving = column_call(parity, strips, taper_a, taper_b)
    arrived = lax.all_to_all(leaving.reshape(256, 16, TILE), ("row", "bl"), 0, 0, tiled=True)
    return row_call(arrived.reshape(64, 4, 16, TILE))


def solution(mesh):
    in_specs = (
        P("bl", "row", None, None, None),
        P("bl", "row", None, None, None, None),
        P("bl", "row", None, None, None),
        P("bl", "row", None),
        P("bl", "row", None),
        P(("row", "bl"), None),
    )
    out_specs = P(None, ("row", "bl"), None)
    return jax.shard_map(body, mesh=mesh, in_specs=in_specs, out_specs=out_specs, check_vma=False)
```

time: 542 us -> 136 us (0.25); the launches traced: 534 us -> 136 us
  waiting for transfers between devices: 203 us -> 22.1 us
  local copies, waits for them, and re-layouts: 115 us -> 4.03 us
  matrix products: 81.7 us -> 0 us
  other arithmetic: 35.7 us -> 0 us
  blocking collectives: 51.7 us -> 79.5 us
  Pallas kernels: 0 us -> 21.7 us
  loops' own time: 20.9 us -> 0 us
  between operations: 13.9 us -> 0.13 us
    reduce_scatter x1 -> x0, waiting for transfers between devices: 178 us -> none  [body(): summed = lax.psum_scatter(band_grid, 'bl', scatter_dimension=1, tiled=True)]
    dot_general x18 -> x0, matrix products: 81.7 us -> none  [the longest x4 20.1 us: complex_einsum(): jnp.einsum(formula, left_im, right_im, precision=precise)]
    all_to_all x1, blocking collectives: 51.7 us -> 79.5 us  [body(): lax.all_to_all(leaving.reshape(256, 16, TILE), ('row', 'bl'), 0, 0, tiled...]
    all_to_all x4 -> x0, local copies, waits for them, and re-layouts: 26 us -> none  [body(): lax.all_to_all(stacked, 'row', split_axis=2, concat_axis=1, tiled=True)]
    all_to_all x1, waiting for transfers between devices: 25.5 us -> 0.01 us  [body(): strips = lax.all_to_all(strips, 'bl', 0, 0, tiled=True)]
    ppermute x0 -> x2, waiting for transfers between devices: none -> 22.1 us  [the longest x1 22.1 us: body(): taper_b = lax.ppermute(taper_b, 'bl', to_b)]
    pallas_call x0 -> x3, Pallas kernels: none -> 21.7 us  [the longest x1 8.76 us: column_call(): pl.pallas_call(column_kernel, out_shape=jax.ShapeDtypeStruct((TILE, 2, 16...]
    another operation x2 -> x0, loops' own time: 20.9 us -> none  [the longest x1 20.7 us: body(): lax.fori_loop(0, slot_count, place_slot, jnp.zeros((2, band_rows, grid_si...]
  transfers between devices with their start and end apart: 2 -> 3, of which waited for: 2 -> 1; matrix products, arithmetic and copies ran while one was open for 0% -> 0% of each run, Pallas kernels for 0% -> 0%
where the time goes in v1:
time: 136 us
  blocking collectives  79.5 us (58%)
  waiting for transfers between devices  22.1 us (16%)
  Pallas kernels  21.7 us (16%)
  starting transfers between devices  8.71 us (6%)
  local copies, waits for them, and re-layouts  4.03 us (3%)
    all_to_all x1, blocking collectives, body(): lax.all_to_all(leaving.reshape(256, 16, TILE), ('row', 'bl'), 0, 0, tiled...  79.5 us
    ppermute x1, waiting for transfers between devices, body(): taper_b = lax.ppermute(taper_b, 'bl', to_b)  22.1 us
    pallas_call x1, Pallas kernels, column_call(): pl.pallas_call(column_kernel, out_shape=jax.ShapeDtypeStruct((TILE, 2, 16...  8.76 us
    pallas_call x1, Pallas kernels, row_call(): pl.pallas_call(row_kernel, out_shape=jax.ShapeDtypeStruct((2, 32, G), F32...  8 us
    all_to_all x1, starting transfers between devices, body(): strips = lax.all_to_all(strips, 'bl', 0, 0, tiled=True)  6.5 us
    pallas_call x1, Pallas kernels, grid_call(): pl.pallas_call(grid_kernel, out_shape=jax.ShapeDtypeStruct((N_BL, 264, TI...  4.9 us
    unnamed x28, local copies, waits for them, and re-layouts  3.95 us
  transfers between devices with their start and end apart: 3, of which 1 were waited for; matrix products, arithmetic and copies ran while one was open for 0% of the time, Pallas kernels for 0%

profile of v1, /device:TPU:1, one launch (start us, length us, event | category | flops | bytes accessed | tf_op | source)
XLA Modules:
  0.0 136.1 jit_solution(14711555673522565549)
XLA Ops:
  0.0 0.0 copy-start.3
  0.0 1.0 copy-done.3
  1.0 0.0 copy-start.9
  1.0 0.8 copy-done.9
  1.8 0.0 copy-start.10
  1.8 0.8 copy-done.10
  2.6 0.0 copy-start.11
  2.6 0.7 copy-done.11
  3.3 0.0 copy-start.12
  3.3 0.7 copy-done.12
  3.9 0.0 copy-start.13
  3.9 4.9 %shard_map.136 = f32[8,264,128]{2,1,0:T(8,128)} custom-call(s32[8]{0:T(128)S(1)} %bitcast.13, s32[8]{0:T(128)S(1)} %bitcast.14, f32[8,2,768]{2,1,0:T(2,128)S(1)} %bitcast.11, f32[8,2,8,768]{3,2,1,0:T(8,128)S(1)} %bitcast.10, s32[8,2,768]{2,1,0:T(2,128)S(1)} %bitcast.12), custom_call_target="tpu_custom_call" | custom-call | tf_op jit(solution)/shard_map/pallas_call | solution.py:124
  8.8 0.0 copy-start.6
  8.8 0.0 copy-start.7
  8.8 0.0 copy-start.8
  8.8 6.5 %all-to-all-start = ((f32[8,264,128]{2,1,0:T(8,128)}), f32[8,264,128]{2,1,0:T(8,128)S(1)}, u32[]{:S(2)}, u32[]{:S(2)}) async-start(f32[8,264,128]{2,1,0:T(8,128)} %shard_map.136), calls=%async_computation | async-start | bytes 2162688 | tf_op jit(solution)/shard_map/all_to_all | solution.py:340
  15.3 0.0 copy-done.13
  15.3 0.1 constant_dynamic-slice_fusion
  15.4 1.5 %collective-permute-start.1 = (f32[16,8192]{1,0:T(8,128)S(1)}, f32[16,8192]{1,0:T(8,128)S(1)}, u32[]{:S(2)}, u32[]{:S(2)}) collective-permute-start(f32[16,8192]{1,0:T(8,128)S(1)} %get-tuple-element.5), channel_id=1, source_target_pairs={{0,32},{32,96},{64,160},{96,224},{128,0},{160,64},{192,128},{224,1... | collective-permute-start | bytes 1572872 | tf_op jit(solution)/shard_map/ppermute | solution.py:336
  16.9 0.7 collective-permute-start
  17.6 22.1 %collective-permute-done.1.taper_b = f32[16,8192]{1,0:T(8,128)S(1)} collective-permute-done((f32[16,8192]{1,0:T(8,128)S(1)}, f32[16,8192]{1,0:T(8,128)S(1)}, u32[]{:S(2)}, u32[]{:S(2)}) %collective-permute-start.1) | collective-permute-done | bytes 524320 | tf_op jit(solution)/shard_map/ppermute | solution.py:336
  39.7 0.0 collective-permute-done.taper_a
  39.7 0.0 all-to-all-done.strips
  39.7 0.0 copy-done.6
  39.7 0.0 copy-done.7
  39.7 0.0 copy-done.8
  39.7 8.8 %shard_map.137 = f32[128,2,16,128]{3,2,1,0:T(8,128)S(1)} custom-call(s32[1]{0:T(128)} %bitcast.parity, f32[8,264,128]{2,1,0:T(8,128)S(1)} %all-to-all-done.strips, f32[16,8192]{1,0:T(8,128)S(1)} %collective-permute-done.taper_a, f32[16,8192]{1,0:T(8,128)S(1)} %collective-permute-done.1.taper_b, f32[2,64,128]{2,1,0:T(8,128)S(1)} %copy-done.8, ...), custom_call_target="tpu_custom_call" | custom-call | tf_op jit(solution)/shard_map/pallas_call | solution.py:214
  48.5 0.0 copy-start
  48.5 0.0 copy-start.1
  48.5 0.0 copy-start.2
  48.5 0.0 copy-start.4
  48.6 0.0 copy-start.5
  48.6 79.5 %all_to_all.10 = f32[256,16,128]{2,1,0:T(8,128)S(1)} all-to-all(f32[256,16,128]{2,1,0:T(8,128)S(1)} %bitcast.9), channel_id=1, replica_groups=mesh['bl'=8,'row'=32] {'row','bl'}, dimensions={0} | all-to-all | bytes 4194304 | tf_op jit(solution)/shard_map/all_to_all | solution.py:343
  128.1 0.0 copy-done
  128.1 0.0 copy-done.1
  128.1 0.0 copy-done.2
  128.1 0.0 copy-done.4
  128.1 0.0 copy-done.5
  128.1 8.0 %shard_map.138 = f32[2,32,8192]{2,1,0:T(8,128)} custom-call(f32[64,4,16,128]{3,2,1,0:T(8,128)S(1)} %bitcast.8, bf16[256,256]{1,0:T(8,128)(2,1)S(1)} %copy-done.5, bf16[256,256]{1,0:T(8,128)(2,1)S(1)} %copy-done.4, f32[4,2,128,128]{3,2,1,0:T(8,128)S(1)} %copy-done.2, bf16[4,256,256]{2,1,0:T(8,128)(2,1)S(1)} %copy-done.1, bf16[4,256,256]{2,1,0:T(8,128)(2,1)S(1)} %copy-done), custom_call_target="tpu_custom_call" | custom-call | tf_op jit(solution)/shard_map/pallas_call | solution.py:311
Async XLA Ops:
  0.0 1.0 copy-start.3
  1.0 0.8 copy-start.9
  1.8 0.8 copy-start.10
  2.6 0.7 copy-start.11
  3.3 0.7 copy-start.12
  3.9 11.4 %copy-start.13 = (f32[32,8192]{1,0:T(8,128)S(1)}, f32[32,8192]{1,0:T(8,128)}, u32[]{:S(2)}) copy-start(f32[32,8192]{1,0:T(8,128)} %param.19) | copy-start | bytes 3145732
  8.8 30.9 %copy-start.6 = (bf16[256,256]{1,0:T(8,128)(2,1)S(1)}, bf16[256,256]{1,0:T(8,128)(2,1)}, u32[]{:S(2)}) copy-start(bf16[256,256]{1,0:T(8,128)(2,1)} %constant.46.clone.wl) | copy-start | bytes 393220
  8.8 30.9 %copy-start.7 = (bf16[256,256]{1,0:T(8,128)(2,1)S(1)}, bf16[256,256]{1,0:T(8,128)(2,1)}, u32[]{:S(2)}) copy-start(bf16[256,256]{1,0:T(8,128)(2,1)} %constant.45.clone.wh) | copy-start | bytes 393220
  8.8 30.9 %copy-start.8 = (f32[2,64,128]{2,1,0:T(8,128)S(1)}, f32[2,64,128]{2,1,0:T(8,128)}, u32[]{:S(2)}) copy-start(f32[2,64,128]{2,1,0:T(8,128)} %constant.44.clone.tw) | copy-start | bytes 196612
  8.8 30.9 %all-to-all-start = ((f32[8,264,128]{2,1,0:T(8,128)}), f32[8,264,128]{2,1,0:T(8,128)S(1)}, u32[]{:S(2)}, u32[]{:S(2)}) async-start(f32[8,264,128]{2,1,0:T(8,128)} %shard_map.136), calls=%async_computation | async-start | bytes 2162688 | tf_op jit(solution)/shard_map/all_to_all | solution.py:340
  15.4 24.3 %collective-permute-start.1 = (f32[16,8192]{1,0:T(8,128)S(1)}, f32[16,8192]{1,0:T(8,128)S(1)}, u32[]{:S(2)}, u32[]{:S(2)}) collective-permute-start(f32[16,8192]{1,0:T(8,128)S(1)} %get-tuple-element.5), channel_id=1, source_target_pairs={{0,32},{32,96},{64,160},{96,224},{128,0},{160,64},{192,128},{224,1... | collective-permute-start | bytes 1572872 | tf_op jit(solution)/shard_map/ppermute | solution.py:336
  16.9 22.8 %collective-permute-start = (f32[16,8192]{1,0:T(8,128)S(1)}, f32[16,8192]{1,0:T(8,128)S(1)}, u32[]{:S(2)}, u32[]{:S(2)}) collective-permute-start(f32[16,8192]{1,0:T(8,128)S(1)} %get-tuple-element.6), channel_id=1, source_target_pairs={{0,0},{32,64},{64,128},{96,192},{128,32},{160,96},{192,160},{224,2... | collective-permute-start | bytes 1572872 | tf_op jit(solution)/shard_map/ppermute | solution.py:335
  48.5 79.6 %copy-start = (bf16[4,256,256]{2,1,0:T(8,128)(2,1)S(1)}, bf16[4,256,256]{2,1,0:T(8,128)(2,1)}, u32[]{:S(2)}) copy-start(bf16[4,256,256]{2,1,0:T(8,128)(2,1)} %constant.51.clone.gl) | copy-start | bytes 1572868
  48.5 79.6 %copy-start.1 = (bf16[4,256,256]{2,1,0:T(8,128)(2,1)S(1)}, bf16[4,256,256]{2,1,0:T(8,128)(2,1)}, u32[]{:S(2)}) copy-start(bf16[4,256,256]{2,1,0:T(8,128)(2,1)} %constant.50.clone.gh) | copy-start | bytes 1572868
  48.5 79.6 %copy-start.2 = (f32[4,2,128,128]{3,2,1,0:T(8,128)S(1)}, f32[4,2,128,128]{3,2,1,0:T(8,128)}, u32[]{:S(2)}) copy-start(f32[4,2,128,128]{3,2,1,0:T(8,128)} %constant.49.clone.tw) | copy-start | bytes 1572868
  48.5 79.6 %copy-start.4 = (bf16[256,256]{1,0:T(8,128)(2,1)S(1)}, bf16[256,256]{1,0:T(8,128)(2,1)}, u32[]{:S(2)}) copy-start(bf16[256,256]{1,0:T(8,128)(2,1)} %constant.48.clone.w1l) | copy-start | bytes 393220
  48.6 79.5 %copy-start.5 = (bf16[256,256]{1,0:T(8,128)(2,1)S(1)}, bf16[256,256]{1,0:T(8,128)(2,1)}, u32[]{:S(2)}) copy-start(bf16[256,256]{1,0:T(8,128)(2,1)} %constant.47.clone.w1h) | copy-start | bytes 393220

commit v2 on v1

--- a/solution.py
+++ b/solution.py
@@ -21,6 +21,7 @@
 COLS = G // TILE
 F32 = jnp.float32
 BF16 = jnp.bfloat16
+HBM = pltpu.MemorySpace.HBM
 NT = (((1,), (1,)), ((), ()))
 
 
@@ -77,9 +78,37 @@
     return (x[0] * cosine + x[1] * sine, x[1] * cosine - x[0] * sine)
 
 
-def grid_kernel(counts, tiles, vis, taps, offs, out):
+def grid_kernel(
+    counts_in, tiles_in, vis_in, taps_in, offs_in, out,
+    counts, tiles, vis, taps, offs, strips, number, sem_few, sem_in, sem_out, sem_num,
+):
+    few = [
+        pltpu.make_async_copy(counts_in, counts, sem_few.at[0]),
+        pltpu.make_async_copy(tiles_in, tiles, sem_few.at[1]),
+        pltpu.make_async_copy(vis_in, vis, sem_few.at[2]),
+        pltpu.make_async_copy(offs_in, offs, sem_few.at[3]),
+    ]
+    for copy in few:
+        copy.start()
+    tap_copies = []
+    for s in range(SLOTS):
+        copy = pltpu.make_async_copy(taps_in.at[s], taps.at[s], sem_in.at[s])
+        copy.start()
+        tap_copies.append(copy)
+    for copy in few:
+        copy.wait()
     sub_index = lax.broadcasted_iota(jnp.int32, (SUP, CAP), 0)
     lane = lax.broadcasted_iota(jnp.int32, (1, CAP), 1)
+    slot_index = lax.broadcasted_iota(jnp.int32, (SLOTS, TILE), 0)
+    numbers = jnp.zeros((SLOTS, TILE), jnp.int32)
+    for s in range(SLOTS):
+        numbers = jnp.where(slot_index == s, tiles[0, s], numbers)
+    number[...] = numbers.astype(F32)
+    leaving = []
+    for d in range(N_BL):
+        copy = pltpu.make_async_copy(number, out.at[d, pl.ds(256, 8), :], sem_num.at[d])
+        copy.start()
+        leaving.append(copy)
 
     def place(block, taken):
         pieces = [jnp.where(taken == x, block, 0.0) for x in range(TILE // SUP)]
@@ -94,8 +123,9 @@
         taken = (first >> 3) + jnp.where(sub_index < shift, 1, 0)
         return value, taken
 
-    def one_slot(s, carry):
-        live = lane < counts[s]
+    for s in range(SLOTS):
+        tap_copies[s].wait()
+        live = lane < counts[0, s]
         value, taken = rotated(s, 0)
         lefts = [split(value * jnp.where(live, vis[s, p : p + 1, :], 0.0)) for p in range(2)]
         left = jnp.concatenate(
@@ -108,37 +138,56 @@
         tile = (prod[:256, :128] + prod[256:, :128]) + (prod[:256, 128:] + prod[256:, 128:])
         for p in range(2):
             for d in range(N_BL):
-                start = p * TILE + d * STRIP
-                out[d, pl.ds(s * 32 + p * STRIP, STRIP), :] = tile[start : start + STRIP]
-        number = jnp.full((1, TILE), tiles[s], jnp.int32).astype(F32)
-        for d in range(N_BL):
-            out[d, pl.ds(256 + s, 1), :] = number
-        return carry
-
-    lax.fori_loop(0, SLOTS, one_slot, 0)
+                start = p * TILE + first_row(d)
+                strips[s, d, p * STRIP : (p + 1) * STRIP, :] = tile[start : start + STRIP]
+        copy = pltpu.make_async_copy(strips.at[s], out.at[:, pl.ds(s * 32, 32), :], sem_out.at[s])
+        copy.start()
+        leaving.append(copy)
+    for copy in leaving:
+        copy.wait()
+
+
+def first_row(d):
+    return (d % 4) * 32 + (d // 4) * STRIP
 
 
 def grid_call(counts, tiles, vis, taps, offs):
-    smem = pl.BlockSpec(memory_space=pltpu.SMEM)
-    vmem = pl.BlockSpec(memory_space=pltpu.VMEM)
+    hbm = pl.BlockSpec(memory_space=HBM)
     return pl.pallas_call(
         grid_kernel,
         out_shape=jax.ShapeDtypeStruct((N_BL, 264, TILE), F32),
-        in_specs=[smem, smem, vmem, vmem, vmem],
-        out_specs=vmem,
-        compiler_params=pltpu.CompilerParams(vmem_limit_bytes=40 << 20),
+        in_specs=[hbm] * 5,
+        out_specs=hbm,
+        scratch_shapes=[
+            pltpu.SMEM((1, SLOTS), jnp.int32),
+            pltpu.SMEM((1, SLOTS), jnp.int32),
+            pltpu.VMEM((SLOTS, 2, CAP), F32),
+            pltpu.VMEM((SLOTS, 2, SUP, CAP), F32),
+            pltpu.VMEM((SLOTS, 2, CAP), jnp.int32),
+            pltpu.VMEM((SLOTS, N_BL, 32, TILE), F32),
+            pltpu.VMEM((SLOTS, TILE), F32),
+            pltpu.SemaphoreType.DMA((4,)),
+            pltpu.SemaphoreType.DMA((SLOTS,)),
+            pltpu.SemaphoreType.DMA((SLOTS,)),
+            pltpu.SemaphoreType.DMA((N_BL,)),
+        ],
+        compiler_params=pltpu.CompilerParams(vmem_limit_bytes=60 << 20),
+        cost_estimate=pl.CostEstimate(flops=4 << 30, bytes_accessed=8 << 20, transcendentals=0),
     )(counts, tiles, vis, taps, offs)
 
 
 def column_kernel(
-    parity, strips, taper_a, taper_b, tw, wh, wl, out,
-    taper, cells, half, xh, xl, ob, number, place, sem_in, sem_out,
+    side, strips, taper_own, taper_in, taper_more, tw, wh, wl, out,
+    taper, cells, half, xh, xl, ob, number, place, sem_in,
 ):
-    par = parity[0]
-    in_a = pltpu.make_async_copy(taper_a, taper.at[par], sem_in.at[0])
-    in_b = pltpu.make_async_copy(taper_b, taper.at[1 - par], sem_in.at[1])
+    mine = side[0]
+    kept = pl.ds(pl.multiple_of(mine * STRIP, STRIP), STRIP)
+    in_a = pltpu.make_async_copy(taper_own.at[kept], taper.at[mine], sem_in.at[0])
+    in_b = pltpu.make_async_copy(taper_in, taper.at[1 - mine, pl.ds(0, 8)], sem_in.at[1])
+    in_c = pltpu.make_async_copy(taper_more, taper.at[1 - mine, pl.ds(8, 8)], sem_in.at[3])
     in_a.start()
     in_b.start()
+    in_c.start()
     number[...] = strips[:, 256:264, :].reshape(64, TILE).astype(jnp.int32)
     to_scalar = pltpu.make_async_copy(number, place, sem_in.at[2])
     to_scalar.start()
@@ -155,7 +204,7 @@
     lax.fori_loop(0, 64, add_strip, 0, unroll=4)
     in_a.wait()
     in_b.wait()
-    copies = []
+    in_c.wait()
     for tr in range(BANDS):
         for a0 in range(8):
             x = []
@@ -187,70 +236,60 @@
             kh = block // 2
             for p in range(2):
                 for m in range(2):
-                    row = (p * 2 + tr) * 4 + (block % 2) * 2 + m
-                    ob[kh * 16 + row] = prod[p * TILE : (p + 1) * TILE, m * TILE : (m + 1) * TILE]
-                    copy = pltpu.make_async_copy(
-                        ob.at[kh * 16 + row], out.at[:, kh, row, :], sem_out.at[kh * 16 + row]
-                    )
-                    copy.start()
-                    copies.append(copy)
-    for copy in copies:
-        copy.wait()
+                    row = tr * 4 + (block % 2) * 2 + m
+                    ob[kh, p, row] = prod[p * TILE : (p + 1) * TILE, m * TILE : (m + 1) * TILE]
+            if tr == 1 and block % 2 == 1:
+                for p in range(2):
+                    out[kh, :, p * 8 : p * 8 + 8, :] = jnp.swapaxes(ob[kh, p], 0, 1)
 
 
 def column_tables():
     k = np.arange(COLS)[:, None]
     y = np.arange(TILE)[None, :]
     turn = np.stack(unit(G, k * y)).astype(np.float32)
-    q = np.arange(TILE)[:, None]
+    zl, r, yh = np.meshgrid(np.arange(2), np.arange(N_ROW), np.arange(2), indexing="ij")
+    q = (r * 4 + zl * 2 + yh).reshape(TILE, 1)
     high, low = halves(real_form(*unit(TILE, q * y)))
     return turn, high, low
 
 
-def column_call(parity, strips, taper_a, taper_b):
+def column_call(side, strips, taper_own, taper_in, taper_more):
     smem = pl.BlockSpec(memory_space=pltpu.SMEM)
     vmem = pl.BlockSpec(memory_space=pltpu.VMEM)
     hbm = pl.BlockSpec(memory_space=pl.ANY)
     return pl.pallas_call(
         column_kernel,
-        out_shape=jax.ShapeDtypeStruct((TILE, 2, 16, TILE), F32),
-        in_specs=[smem, vmem, hbm, hbm, vmem, vmem, vmem],
-        out_specs=hbm,
+        out_shape=jax.ShapeDtypeStruct((2, TILE, 16, TILE), F32),
+        in_specs=[smem, vmem, hbm, hbm, hbm, vmem, vmem, vmem],
+        out_specs=vmem,
         scratch_shapes=[
             pltpu.VMEM((2, STRIP, G), F32),
             pltpu.VMEM((BANDS * COLS, 32, TILE), F32),
             pltpu.VMEM((64, 32, TILE), F32),
             pltpu.VMEM((BANDS, 1024, 256), BF16),
             pltpu.VMEM((BANDS, 1024, 256), BF16),
-            pltpu.VMEM((32, TILE, TILE), F32),
+            pltpu.VMEM((2, 2, 8, TILE, TILE), F32),
             pltpu.VMEM((64, TILE), jnp.int32),
             pltpu.SMEM((64, TILE), jnp.int32),
-            pltpu.SemaphoreType.DMA((3,)),
-            pltpu.SemaphoreType.DMA((32,)),
+            pltpu.SemaphoreType.DMA((4,)),
         ],
         compiler_params=pltpu.CompilerParams(vmem_limit_bytes=40 << 20),
-    )(parity, strips, taper_a, taper_b, *column_tables())
-
-
-def row_kernel(arrived, w1h, w1l, tw, gh, gl, out, x, at, bh, bl, sem):
-    copies = []
+    )(side, strips, taper_own, taper_in, taper_more, *column_tables())
+
+
+def row_kernel(arrived, w1h, w1l, tw, gh, gl, out, xh, xl, at, bh, bl):
     for dl in range(4):
-        for s in range(16):
-            pt, mb = s // 4, s % 4
-            copy = pltpu.make_async_copy(
-                arrived.at[:, dl, s, :],
-                x.at[dl, pl.ds(pt * 64, 64), pl.ds(mb * TILE, TILE)],
-                sem.at[dl * 16 + s],
-            )
-            copy.start()
-            copies.append(copy)
-    for dl in range(4):
-        for copy in copies[dl * 16 : dl * 16 + 16]:
-            copy.wait()
-        high, low = split(x[dl])
-        prod = jnp.dot(w1h[...], high, preferred_element_type=F32)
-        prod += jnp.dot(w1l[...], high, preferred_element_type=F32)
-        prod += jnp.dot(w1h[...], low, preferred_element_type=F32)
+        for half in range(2):
+            rows = jnp.swapaxes(arrived[dl, :, half * 8 : half * 8 + 8, :], 0, 1)
+            for t in range(8):
+                to = (half * 2 + t // 4) * 64
+                lanes = (t % 4) * TILE
+                high, low = split(rows[t])
+                xh[dl, to : to + 64, lanes : lanes + TILE] = high
+                xl[dl, to : to + 64, lanes : lanes + TILE] = low
+        prod = jnp.dot(w1h[...], xh[dl], preferred_element_type=F32)
+        prod += jnp.dot(w1l[...], xh[dl], preferred_element_type=F32)
+        prod += jnp.dot(w1h[...], xl[dl], preferred_element_type=F32)
         at[dl] = prod
 
     def radix(step, carry):
@@ -287,8 +326,8 @@
 
 def row_tables():
     ka = np.arange(TILE)[:, None]
-    tr, r, dh = np.meshgrid(np.arange(2), np.arange(N_ROW), np.arange(2), indexing="ij")
-    coarse = (r * 4 + tr * 2 + dh).reshape(1, TILE)
+    tr, r, yh = np.meshgrid(np.arange(2), np.arange(N_ROW), np.arange(2), indexing="ij")
+    coarse = (r * 4 + tr * 2 + yh).reshape(1, TILE)
     w1h, w1l = halves(real_form(*unit(TILE, ka * coarse)))
     fine = np.arange(TILE)[None, :] % 16
     turn = np.stack([np.stack(unit(G, ka * (dl * 16 + fine))) for dl in range(4)])
@@ -307,41 +346,48 @@
 
 def row_call(arrived):
     vmem = pl.BlockSpec(memory_space=pltpu.VMEM)
-    hbm = pl.BlockSpec(memory_space=pl.ANY)
     return pl.pallas_call(
         row_kernel,
         out_shape=jax.ShapeDtypeStruct((2, 32, G), F32),
-        in_specs=[hbm, vmem, vmem, vmem, vmem, vmem],
+        in_specs=[vmem, vmem, vmem, vmem, vmem, vmem],
         out_specs=vmem,
         scratch_shapes=[
-            pltpu.VMEM((4, 256, 512), F32),
+            pltpu.VMEM((4, 256, 512), BF16),
+            pltpu.VMEM((4, 256, 512), BF16),
             pltpu.VMEM((4, 256, 512), F32),
             pltpu.VMEM((4, 512, 256), BF16),
             pltpu.VMEM((4, 512, 256), BF16),
-            pltpu.SemaphoreType.DMA((64,)),
         ],
         compiler_params=pltpu.CompilerParams(vmem_limit_bytes=40 << 20),
     )(arrived, *row_tables())
 
 
 def body(visibilities, kernels, offsets, counts, slot_tiles, taper):
-    me = lax.axis_index("bl")
-    low = me < N_BL // 2
-    first = jnp.where(low, 0, STRIP)
-    taper_a = lax.dynamic_slice(taper, (first, 0), (STRIP, G))
-    taper_b = lax.dynamic_slice(taper, (STRIP - first, 0), (STRIP, G))
-    to_a = [(s, (2 * s + (s >= 4)) % 8) for s in range(N_BL)]
-    to_b = [(s, (2 * s + (s < 4)) % 8) for s in range(N_BL)]
-    taper_a = lax.ppermute(taper_a, "bl", to_a)
-    taper_b = lax.ppermute(taper_b, "bl", to_b)
-    strips = grid_call(
-        counts[0, 0], slot_tiles[0, 0], visibilities[0, 0], kernels[0, 0], offsets[0, 0]
+    side = lax.axis_index("bl") // 4
+    swap = [(s, (s + 4) % 8) for s in range(N_BL)]
+    given = lax.dynamic_slice(taper, ((1 - side) * STRIP, 0), (8, G))
+    taper_in = lax.ppermute(given, "bl", swap)
+    strips = grid_call(counts[0], slot_tiles[0], visibilities[0, 0], kernels[0, 0], offsets[0, 0])
+    strips, taper_in = lax.optimization_barrier((strips, taper_in))
+    given = lax.dynamic_slice(taper, ((1 - side) * STRIP + 8, 0), (8, G))
+    taper_more = lax.ppermute(given, "bl", swap)
+    strips = lax.all_to_all(strips, "bl", 0, 0, tiled=True)
+    side = side.reshape(1).astype(jnp.int32)
+    leaving = column_call(side, strips, taper, taper_in, taper_more)
+    arrived = lax.all_to_all(
+        leaving.reshape(256, 16, TILE), ("bl", "row"), 0, 0, axis_index_groups=members(), tiled=True
     )
-    strips = lax.all_to_all(strips, "bl", 0, 0, tiled=True)
-    parity = (me % 2).reshape(1).astype(jnp.int32)
-    leaving = column_call(parity, strips, taper_a, taper_b)
-    arrived = lax.all_to_all(leaving.reshape(256, 16, TILE), ("row", "bl"), 0, 0, tiled=True)
-    return row_call(arrived.reshape(64, 4, 16, TILE))
+    return row_call(arrived.reshape(4, 64, 16, TILE))
+
+
+def members():
+    group = []
+    for yl in range(2):
+        for zl in range(2):
+            for r in range(N_ROW):
+                for yh in range(2):
+                    group.append((zl * 4 + yh * 2 + yl) * N_ROW + r)
+    return [group]
 
 
 def solution(mesh):

time: 136 us -> 111 us (0.82)
  blocking collectives: 79.5 us -> 69.3 us
  Pallas kernels: 21.7 us -> 15.6 us
  waiting for transfers between devices: 22.1 us -> 16.4 us
  local copies, waits for them, and re-layouts: 4.03 us -> 1.12 us
    all_to_all x1, blocking collectives: 79.5 us -> 69.3 us  [body(): lax.all_to_all(leaving.reshape(256, 16, TILE), ('bl', 'row'), 0, 0, axis_...]
    ppermute x2, waiting for transfers between devices: 22.1 us -> 16.4 us  [the longest x1 16.4 us: body(): taper_more = lax.ppermute(given, 'bl', swap)]
    pallas_call x1, Pallas kernels: 8.76 us -> 4.15 us  [column_call(): pl.pallas_call(column_kernel, out_shape=jax.ShapeDtypeStruct((2, TILE, 16...]
    unnamed x28 -> x18, local copies, waits for them, and re-layouts: 3.95 us -> 0.06 us
    pallas_call x1, Pallas kernels: 8 us -> 4.82 us  [row_call(): pl.pallas_call(row_kernel, out_shape=jax.ShapeDtypeStruct((2, 32, G), F32...]
    all_to_all x1, starting transfers between devices: 6.5 us -> 4.35 us  [body(): strips = lax.all_to_all(strips, 'bl', 0, 0, tiled=True)]
    ppermute x2, starting transfers between devices: 2.21 us -> 4.02 us  [the longest x1 2.55 us: body(): taper_in = lax.ppermute(given, 'bl', swap)]
    pallas_call x1, Pallas kernels: 4.9 us -> 6.66 us  [grid_call(): pl.pallas_call(grid_kernel, out_shape=jax.ShapeDtypeStruct((N_BL, 264, TI...]
  transfers between devices with their start and end apart: 3 -> 3, of which waited for: 1 -> 1; matrix products, arithmetic and copies ran while one was open for 0% -> 0% of each run, Pallas kernels for 0% -> 6%
where the time goes in v2:
time: 111 us
  blocking collectives  69.3 us (62%)
  waiting for transfers between devices  16.4 us (15%)
  Pallas kernels  15.6 us (14%)
  starting transfers between devices  8.36 us (8%)
  local copies, waits for them, and re-layouts  1.12 us (1%)
    all_to_all x1, blocking collectives, body(): lax.all_to_all(leaving.reshape(256, 16, TILE), ('bl', 'row'), 0, 0, axis_...  69.3 us
    ppermute x1, waiting for transfers between devices, body(): taper_more = lax.ppermute(given, 'bl', swap)  16.4 us
    pallas_call x1, Pallas kernels, grid_call(): pl.pallas_call(grid_kernel, out_shape=jax.ShapeDtypeStruct((N_BL, 264, TI...  6.66 us
    pallas_call x1, Pallas kernels, row_call(): pl.pallas_call(row_kernel, out_shape=jax.ShapeDtypeStruct((2, 32, G), F32...  4.82 us
    all_to_all x1, starting transfers between devices, body(): strips = lax.all_to_all(strips, 'bl', 0, 0, tiled=True)  4.35 us
    pallas_call x1, Pallas kernels, column_call(): pl.pallas_call(column_kernel, out_shape=jax.ShapeDtypeStruct((2, TILE, 16...  4.15 us
    ppermute x1, starting transfers between devices, body(): taper_in = lax.ppermute(given, 'bl', swap)  2.55 us
  transfers between devices with their start and end apart: 3, of which 1 were waited for; matrix products, arithmetic and copies ran while one was open for 0% of the time, Pallas kernels for 6%

profile of v2, /device:TPU:1, one launch (start us, length us, event | category | flops | bytes accessed | tf_op | source)
XLA Modules:
  0.0 110.9 jit_solution(7773093300896680219)
XLA Ops:
  0.0 1.1 constant_dynamic-slice_fusion
  1.1 2.6 %collective-permute-start = (f32[8,8192]{1,0:T(8,128)S(1)}, f32[8,8192]{1,0:T(8,128)S(1)}, u32[]{:S(2)}, u32[]{:S(2)}) collective-permute-start(f32[8,8192]{1,0:T(8,128)S(1)} %get-tuple-element.10), channel_id=1, source_target_pairs={{0,128},{32,160},{64,192},{96,224},{128,0},{160,32},{192,64},{224,... | collective-permute-start | bytes 786440 | tf_op jit(solution)/shard_map/ppermute | solution.py:369
  3.6 6.7 %shard_map.136 = f32[8,264,128]{2,1,0:T(8,128)} custom-call(s32[1,8]{1,0:T(1,128)} %bitcast.13, s32[1,8]{1,0:T(1,128)} %bitcast.14, f32[8,2,768]{2,1,0:T(2,128)} %bitcast.11, f32[8,2,8,768]{3,2,1,0:T(8,128)} %bitcast.10, s32[8,2,768]{2,1,0:T(2,128)} %bitcast.12), custom_call_target="tpu_custom_call" | custom-call | flops 4294967296 | bytes 8388608 | tf_op jit(solution)/shard_map/pallas_call | solution.py:156
  10.3 0.0 copy-start
  10.3 0.0 copy-start.6
  10.3 0.0 copy-start.7
  10.3 0.0 copy-start.8
  10.3 0.0 collective-permute-done.taper_in
  10.4 4.3 %all-to-all-start = ((f32[8,264,128]{2,1,0:T(8,128)}), f32[8,264,128]{2,1,0:T(8,128)S(1)}, u32[]{:S(2)}, u32[]{:S(2)}) async-start(f32[8,264,128]{2,1,0:T(8,128)} %shard_map.136), calls=%async_computation | async-start | bytes 2162688 | tf_op jit(solution)/shard_map/all_to_all | solution.py:374
  14.7 1.5 %collective-permute-start.1 = (f32[8,8192]{1,0:T(8,128)S(1)}, f32[8,8192]{1,0:T(8,128)S(1)}, u32[]{:S(2)}, u32[]{:S(2)}) collective-permute-start(f32[8,8192]{1,0:T(8,128)S(1)} %get-tuple-element.9), channel_id=1, source_target_pairs={{0,128},{32,160},{64,192},{96,224},{128,0},{160,32},{192,64},{224,... | collective-permute-start | bytes 786440 | tf_op jit(solution)/shard_map/ppermute | solution.py:373
  16.2 16.4 %collective-permute-done.1.taper_more = f32[8,8192]{1,0:T(8,128)S(1)} collective-permute-done((f32[8,8192]{1,0:T(8,128)S(1)}, f32[8,8192]{1,0:T(8,128)S(1)}, u32[]{:S(2)}, u32[]{:S(2)}) %collective-permute-start.1) | collective-permute-done | bytes 262176 | tf_op jit(solution)/shard_map/ppermute | solution.py:373
  32.6 0.0 all-to-all-done.strips
  32.6 0.0 copy-done
  32.6 0.0 copy-done.6
  32.6 0.0 copy-done.7
  32.6 0.0 copy-done.8
  32.6 4.1 %shard_map.137 = f32[2,128,16,128]{3,2,1,0:T(8,128)S(1)} custom-call(s32[1]{0:T(128)} %bitcast.side, f32[8,264,128]{2,1,0:T(8,128)S(1)} %all-to-all-done.strips, f32[32,8192]{1,0:T(8,128)S(1)} %copy-done, f32[8,8192]{1,0:T(8,128)S(1)} %collective-permute-done.taper_in, f32[8,8192]{1,0:T(8,128)S(1)} %collective-permute-done.1.taper_more, ...), custom_call_target="tpu_custom_call" | custom-call | tf_op jit(solution)/shard_map/pallas_call | solution.py:260
  36.7 0.0 copy-start.1
  36.8 0.0 copy-start.2
  36.8 0.0 copy-start.3
  36.8 0.0 copy-start.4
  36.8 0.0 copy-start.5
  36.8 69.3 %all_to_all.10 = f32[256,16,128]{2,1,0:T(8,128)S(1)} all-to-all(f32[256,16,128]{2,1,0:T(8,128)S(1)} %bitcast.9), channel_id=1, replica_groups={{0,64,1,65,2,66,3,67,4,68,5,69,6,70,7,71,8,72,9,73,10,74,11,75,12,76,13..., dimensions={0} | all-to-all | bytes 4194304 | tf_op jit(solution)/shard_map/all_to_all | solution.py:377
  106.1 0.0 copy-done.1
  106.1 0.0 copy-done.2
  106.1 0.0 copy-done.3
  106.1 0.0 copy-done.4
  106.1 0.0 copy-done.5
  106.1 4.8 %shard_map.138 = f32[2,32,8192]{2,1,0:T(8,128)} custom-call(f32[4,64,16,128]{3,2,1,0:T(8,128)S(1)} %bitcast.8, bf16[256,256]{1,0:T(8,128)(2,1)S(1)} %copy-done.5, bf16[256,256]{1,0:T(8,128)(2,1)S(1)} %copy-done.4, f32[4,2,128,128]{3,2,1,0:T(8,128)S(1)} %copy-done.3, bf16[4,256,256]{2,1,0:T(8,128)(2,1)S(1)} %copy-done.2, bf16[4,256,256]{2,1,0:T(8,128)(2,1)S(1)} %copy-done.1), custom_call_target="tpu_custom_call" | custom-call | tf_op jit(solution)/shard_map/pallas_call | solution.py:349
Async XLA Ops:
  1.1 9.3 %collective-permute-start = (f32[8,8192]{1,0:T(8,128)S(1)}, f32[8,8192]{1,0:T(8,128)S(1)}, u32[]{:S(2)}, u32[]{:S(2)}) collective-permute-start(f32[8,8192]{1,0:T(8,128)S(1)} %get-tuple-element.10), channel_id=1, source_target_pairs={{0,128},{32,160},{64,192},{96,224},{128,0},{160,32},{192,64},{224,... | collective-permute-start | bytes 786440 | tf_op jit(solution)/shard_map/ppermute | solution.py:369
  10.3 22.3 %copy-start = (f32[32,8192]{1,0:T(8,128)S(1)}, f32[32,8192]{1,0:T(8,128)}, u32[]{:S(2)}) copy-start(f32[32,8192]{1,0:T(8,128)} %taper_own.1) | copy-start | bytes 3145732
  10.3 22.3 %copy-start.6 = (bf16[256,256]{1,0:T(8,128)(2,1)S(1)}, bf16[256,256]{1,0:T(8,128)(2,1)}, u32[]{:S(2)}) copy-start(bf16[256,256]{1,0:T(8,128)(2,1)} %constant.50.clone.wl) | copy-start | bytes 393220
  10.3 22.2 %copy-start.7 = (bf16[256,256]{1,0:T(8,128)(2,1)S(1)}, bf16[256,256]{1,0:T(8,128)(2,1)}, u32[]{:S(2)}) copy-start(bf16[256,256]{1,0:T(8,128)(2,1)} %constant.49.clone.wh) | copy-start | bytes 393220
  10.3 22.2 %copy-start.8 = (f32[2,64,128]{2,1,0:T(8,128)S(1)}, f32[2,64,128]{2,1,0:T(8,128)}, u32[]{:S(2)}) copy-start(f32[2,64,128]{2,1,0:T(8,128)} %constant.48.clone.tw) | copy-start | bytes 196612
  10.4 22.2 %all-to-all-start = ((f32[8,264,128]{2,1,0:T(8,128)}), f32[8,264,128]{2,1,0:T(8,128)S(1)}, u32[]{:S(2)}, u32[]{:S(2)}) async-start(f32[8,264,128]{2,1,0:T(8,128)} %shard_map.136), calls=%async_computation | async-start | bytes 2162688 | tf_op jit(solution)/shard_map/all_to_all | solution.py:374
  14.7 17.9 %collective-permute-start.1 = (f32[8,8192]{1,0:T(8,128)S(1)}, f32[8,8192]{1,0:T(8,128)S(1)}, u32[]{:S(2)}, u32[]{:S(2)}) collective-permute-start(f32[8,8192]{1,0:T(8,128)S(1)} %get-tuple-element.9), channel_id=1, source_target_pairs={{0,128},{32,160},{64,192},{96,224},{128,0},{160,32},{192,64},{224,... | collective-permute-start | bytes 786440 | tf_op jit(solution)/shard_map/ppermute | solution.py:373
  36.7 69.4 %copy-start.1 = (bf16[4,256,256]{2,1,0:T(8,128)(2,1)S(1)}, bf16[4,256,256]{2,1,0:T(8,128)(2,1)}, u32[]{:S(2)}) copy-start(bf16[4,256,256]{2,1,0:T(8,128)(2,1)} %constant.55.clone.gl) | copy-start | bytes 1572868
  36.8 69.3 %copy-start.2 = (bf16[4,256,256]{2,1,0:T(8,128)(2,1)S(1)}, bf16[4,256,256]{2,1,0:T(8,128)(2,1)}, u32[]{:S(2)}) copy-start(bf16[4,256,256]{2,1,0:T(8,128)(2,1)} %constant.54.clone.gh) | copy-start | bytes 1572868
  36.8 69.3 %copy-start.3 = (f32[4,2,128,128]{3,2,1,0:T(8,128)S(1)}, f32[4,2,128,128]{3,2,1,0:T(8,128)}, u32[]{:S(2)}) copy-start(f32[4,2,128,128]{3,2,1,0:T(8,128)} %constant.53.clone.tw) | copy-start | bytes 1572868
  36.8 69.3 %copy-start.4 = (bf16[256,256]{1,0:T(8,128)(2,1)S(1)}, bf16[256,256]{1,0:T(8,128)(2,1)}, u32[]{:S(2)}) copy-start(bf16[256,256]{1,0:T(8,128)(2,1)} %constant.52.clone.w1l) | copy-start | bytes 393220
  36.8 69.3 %copy-start.5 = (bf16[256,256]{1,0:T(8,128)(2,1)S(1)}, bf16[256,256]{1,0:T(8,128)(2,1)}, u32[]{:S(2)}) copy-start(bf16[256,256]{1,0:T(8,128)(2,1)} %constant.51.clone.w1h) | copy-start | bytes 393220

commit v3 on v2

--- a/solution.py
+++ b/solution.py
@@ -79,9 +79,11 @@
 
 
 def grid_kernel(
-    counts_in, tiles_in, vis_in, taps_in, offs_in, out,
-    counts, tiles, vis, taps, offs, strips, number, sem_few, sem_in, sem_out, sem_num,
+    me, counts_in, tiles_in, vis_in, taps_in, offs_in,
+    out0, out1, out2, out3, out4, out5, out6, out7,
+    counts, tiles, vis, taps, offs, strips, sem_few, sem_in, sem_out,
 ):
+    outs = [out0, out1, out2, out3, out4, out5, out6, out7]
     few = [
         pltpu.make_async_copy(counts_in, counts, sem_few.at[0]),
         pltpu.make_async_copy(tiles_in, tiles, sem_few.at[1]),
@@ -103,12 +105,9 @@
     numbers = jnp.zeros((SLOTS, TILE), jnp.int32)
     for s in range(SLOTS):
         numbers = jnp.where(slot_index == s, tiles[0, s], numbers)
-    number[...] = numbers.astype(F32)
+    for block in range(N_BL):
+        strips[block, 32] = numbers.astype(F32)
     leaving = []
-    for d in range(N_BL):
-        copy = pltpu.make_async_copy(number, out.at[d, pl.ds(256, 8), :], sem_num.at[d])
-        copy.start()
-        leaving.append(copy)
 
     def place(block, taken):
         pieces = [jnp.where(taken == x, block, 0.0) for x in range(TILE // SUP)]
@@ -137,81 +136,85 @@
         prod = lax.dot_general(left, right, NT, preferred_element_type=F32)
         tile = (prod[:256, :128] + prod[256:, :128]) + (prod[:256, 128:] + prod[256:, 128:])
         for p in range(2):
-            for d in range(N_BL):
-                start = p * TILE + first_row(d)
-                strips[s, d, p * STRIP : (p + 1) * STRIP, :] = tile[start : start + STRIP]
-        copy = pltpu.make_async_copy(strips.at[s], out.at[:, pl.ds(s * 32, 32), :], sem_out.at[s])
-        copy.start()
-        leaving.append(copy)
+            for block in range(N_BL):
+                start = p * TILE + block * STRIP
+                to = s * 4 + p * 2
+                strips[block, to : to + 2] = tile[start : start + STRIP].reshape(2, 8, TILE)
+        if s % 4 == 3:
+            part = pl.ds(s // 4 * 16, 16 + s // 7)
+            for step in range(N_BL):
+                other = me[0] ^ step
+                copy = pltpu.make_async_copy(
+                    strips.at[(other & 3) * 2 + (other >> 2), part],
+                    outs[step].at[part],
+                    sem_out.at[s // 4 * N_BL + step],
+                )
+                copy.start()
+                leaving.append(copy)
     for copy in leaving:
         copy.wait()
 
 
-def first_row(d):
-    return (d % 4) * 32 + (d // 4) * STRIP
-
-
-def grid_call(counts, tiles, vis, taps, offs):
+def grid_call(me, counts, tiles, vis, taps, offs):
     hbm = pl.BlockSpec(memory_space=HBM)
     return pl.pallas_call(
         grid_kernel,
-        out_shape=jax.ShapeDtypeStruct((N_BL, 264, TILE), F32),
-        in_specs=[hbm] * 5,
-        out_specs=hbm,
+        out_shape=[jax.ShapeDtypeStruct((33, 8, TILE), F32)] * N_BL,
+        in_specs=[pl.BlockSpec(memory_space=pltpu.SMEM)] + [hbm] * 5,
+        out_specs=[hbm] * N_BL,
         scratch_shapes=[
             pltpu.SMEM((1, SLOTS), jnp.int32),
             pltpu.SMEM((1, SLOTS), jnp.int32),
             pltpu.VMEM((SLOTS, 2, CAP), F32),
             pltpu.VMEM((SLOTS, 2, SUP, CAP), F32),
             pltpu.VMEM((SLOTS, 2, CAP), jnp.int32),
-            pltpu.VMEM((SLOTS, N_BL, 32, TILE), F32),
-            pltpu.VMEM((SLOTS, TILE), F32),
+            pltpu.VMEM((N_BL, 33, 8, TILE), F32),
             pltpu.SemaphoreType.DMA((4,)),
             pltpu.SemaphoreType.DMA((SLOTS,)),
-            pltpu.SemaphoreType.DMA((SLOTS,)),
-            pltpu.SemaphoreType.DMA((N_BL,)),
+            pltpu.SemaphoreType.DMA((2 * N_BL,)),
         ],
         compiler_params=pltpu.CompilerParams(vmem_limit_bytes=60 << 20),
         cost_estimate=pl.CostEstimate(flops=4 << 30, bytes_accessed=8 << 20, transcendentals=0),
-    )(counts, tiles, vis, taps, offs)
+    )(me, counts, tiles, vis, taps, offs)
 
 
 def column_kernel(
-    side, strips, taper_own, taper_in, taper_more, tw, wh, wl, out,
-    taper, cells, half, xh, xl, ob, number, place, sem_in,
+    side, in_own, in1, in2, in3, in4, in5, in6, in7, taper_own, taper_in, tw, wh, wl, out,
+    taper, in0, cells, half, xh, xl, ob, number, place, sem_in,
 ):
     mine = side[0]
     kept = pl.ds(pl.multiple_of(mine * STRIP, STRIP), STRIP)
     in_a = pltpu.make_async_copy(taper_own.at[kept], taper.at[mine], sem_in.at[0])
-    in_b = pltpu.make_async_copy(taper_in, taper.at[1 - mine, pl.ds(0, 8)], sem_in.at[1])
-    in_c = pltpu.make_async_copy(taper_more, taper.at[1 - mine, pl.ds(8, 8)], sem_in.at[3])
+    in_b = pltpu.make_async_copy(taper_in, taper.at[1 - mine], sem_in.at[1])
     in_a.start()
     in_b.start()
-    in_c.start()
-    number[...] = strips[:, 256:264, :].reshape(64, TILE).astype(jnp.int32)
+    in_d = pltpu.make_async_copy(in_own, in0, sem_in.at[3])
+    in_d.start()
+    strips = [in0, in1, in2, in3, in4, in5, in6, in7]
+    for block in range(N_BL):
+        rows = slice(block * SLOTS, (block + 1) * SLOTS)
+        if block == 0:
+            cells[...] = jnp.zeros_like(cells)
+            in_d.wait()
+        number[rows, :] = strips[block][32].astype(jnp.int32)
     to_scalar = pltpu.make_async_copy(number, place, sem_in.at[2])
     to_scalar.start()
-    cells[...] = jnp.zeros_like(cells)
     to_scalar.wait()
 
-    def add_strip(step, carry):
-        tile = place[step, 0]
-        start = pl.multiple_of((step % SLOTS) * 32, 32)
-        rows = strips[step // SLOTS, pl.ds(start, 32), :]
-        cells[tile] = cells[tile] + rows
-        return carry
-
-    lax.fori_loop(0, 64, add_strip, 0, unroll=4)
+    for block in range(N_BL):
+        for slot in range(SLOTS):
+            tile = place[block * SLOTS + slot, 0]
+            cells[tile] = cells[tile] + strips[block][slot * 4 : slot * 4 + 4]
     in_a.wait()
     in_b.wait()
-    in_c.wait()
     for tr in range(BANDS):
         for a0 in range(8):
             x = []
             for a1 in range(8):
                 a = a1 * 8 + a0
                 t = taper[tr, :, a * TILE : (a + 1) * TILE]
-                x.append((cells[tr * COLS + a, 0:16] * t, cells[tr * COLS + a, 16:32] * t))
+                z = cells[tr * COLS + a].reshape(2, STRIP, TILE)
+                x.append((z[0] * t, z[1] * t))
             for k0, y in enumerate(dft8(x)):
                 if a0 * k0:
                     c, s = unit(64, a0 * k0)
@@ -253,18 +256,19 @@
     return turn, high, low
 
 
-def column_call(side, strips, taper_own, taper_in, taper_more):
+def column_call(side, strips, taper_own, taper_in):
     smem = pl.BlockSpec(memory_space=pltpu.SMEM)
     vmem = pl.BlockSpec(memory_space=pltpu.VMEM)
     hbm = pl.BlockSpec(memory_space=pl.ANY)
     return pl.pallas_call(
         column_kernel,
         out_shape=jax.ShapeDtypeStruct((2, TILE, 16, TILE), F32),
-        in_specs=[smem, vmem, hbm, hbm, hbm, vmem, vmem, vmem],
+        in_specs=[smem, hbm] + [vmem] * (N_BL - 1) + [hbm, hbm, vmem, vmem, vmem],
         out_specs=vmem,
         scratch_shapes=[
             pltpu.VMEM((2, STRIP, G), F32),
-            pltpu.VMEM((BANDS * COLS, 32, TILE), F32),
+            pltpu.VMEM((33, 8, TILE), F32),
+            pltpu.VMEM((BANDS * COLS, 4, 8, TILE), F32),
             pltpu.VMEM((64, 32, TILE), F32),
             pltpu.VMEM((BANDS, 1024, 256), BF16),
             pltpu.VMEM((BANDS, 1024, 256), BF16),
@@ -274,7 +278,7 @@
             pltpu.SemaphoreType.DMA((4,)),
         ],
         compiler_params=pltpu.CompilerParams(vmem_limit_bytes=40 << 20),
-    )(side, strips, taper_own, taper_in, taper_more, *column_tables())
+    )(side, *strips, taper_own, taper_in, *column_tables())
 
 
 def row_kernel(arrived, w1h, w1l, tw, gh, gl, out, xh, xl, at, bh, bl):
@@ -363,17 +367,22 @@
 
 
 def body(visibilities, kernels, offsets, counts, slot_tiles, taper):
-    side = lax.axis_index("bl") // 4
-    swap = [(s, (s + 4) % 8) for s in range(N_BL)]
-    given = lax.dynamic_slice(taper, ((1 - side) * STRIP, 0), (8, G))
+    me = lax.axis_index("bl")
+    side = me // 4
+    swap = [(s, s ^ 4) for s in range(N_BL)]
+    given = lax.dynamic_slice(taper, ((1 - side) * STRIP, 0), (STRIP, G))
     taper_in = lax.ppermute(given, "bl", swap)
-    strips = grid_call(counts[0], slot_tiles[0], visibilities[0, 0], kernels[0, 0], offsets[0, 0])
-    strips, taper_in = lax.optimization_barrier((strips, taper_in))
-    given = lax.dynamic_slice(taper, ((1 - side) * STRIP + 8, 0), (8, G))
-    taper_more = lax.ppermute(given, "bl", swap)
-    strips = lax.all_to_all(strips, "bl", 0, 0, tiled=True)
+    strips = grid_call(
+        me.reshape(1).astype(jnp.int32), counts[0], slot_tiles[0], visibilities[0, 0], kernels[0, 0], offsets[0, 0]
+    )
+    far, taper_in = lax.optimization_barrier((list(strips[4:]), taper_in))
+    blocks = list(strips[:4]) + far
+    strips = [blocks[0]] + [
+        lax.ppermute(blocks[step], "bl", [(s, s ^ step) for s in range(N_BL)])
+        for step in range(1, N_BL)
+    ]
     side = side.reshape(1).astype(jnp.int32)
-    leaving = column_call(side, strips, taper, taper_in, taper_more)
+    leaving = column_call(side, strips, taper, taper_in)
     arrived = lax.all_to_all(
         leaving.reshape(256, 16, TILE), ("bl", "row"), 0, 0, axis_index_groups=members(), tiled=True
     )

time: 111 us -> 108 us (0.973)
  waiting for transfers between devices: 16.4 us -> 9 us
  starting transfers between devices: 8.36 us -> 13.2 us
  blocking collectives: 69.3 us -> 67.2 us
    ppermute x1 -> x7, starting transfers between devices: 1.46 us -> 10.7 us  [body(): lax.ppermute(blocks[step], 'bl', [(s, s ^ step) for s in range(N_BL)])]
    ppermute x1 -> x7, waiting for transfers between devices: 16.4 us -> 8.99 us  [body(): lax.ppermute(blocks[step], 'bl', [(s, s ^ step) for s in range(N_BL)])]
    all_to_all x1 -> x0, starting transfers between devices: 4.35 us -> none  [body(): strips = lax.all_to_all(strips, 'bl', 0, 0, tiled=True)]
    all_to_all x1, blocking collectives: 69.3 us -> 67.2 us  [body(): lax.all_to_all(leaving.reshape(256, 16, TILE), ('bl', 'row'), 0, 0, axis_...]
  transfers between devices with their start and end apart: 3 -> 8, of which waited for: 1 -> 4; matrix products, arithmetic and copies ran while one was open for 0% -> 0% of each run, Pallas kernels for 6% -> 6%
where the time goes in v3:
time: 108 us; the launch traced here: 107 us
  blocking collectives  67.2 us (62%)
  Pallas kernels  15.7 us (15%)
  starting transfers between devices  13.2 us (12%)
  waiting for transfers between devices  9 us (8%)
  local copies, waits for them, and re-layouts  2.03 us (2%)
    all_to_all x1, blocking collectives, body(): lax.all_to_all(leaving.reshape(256, 16, TILE), ('bl', 'row'), 0, 0, axis_...  67.2 us
    ppermute x7, starting transfers between devices, body(): lax.ppermute(blocks[step], 'bl', [(s, s ^ step) for s in range(N_BL)])  10.7 us
    ppermute x7, waiting for transfers between devices, body(): lax.ppermute(blocks[step], 'bl', [(s, s ^ step) for s in range(N_BL)])  8.99 us
    pallas_call x1, Pallas kernels, grid_call(): pl.pallas_call(grid_kernel, out_shape=[jax.ShapeDtypeStruct((33, 8, TILE)...  6.91 us
    pallas_call x1, Pallas kernels, row_call(): pl.pallas_call(row_kernel, out_shape=jax.ShapeDtypeStruct((2, 32, G), F32...  4.83 us
    pallas_call x1, Pallas kernels, column_call(): pl.pallas_call(column_kernel, out_shape=jax.ShapeDtypeStruct((2, TILE, 16...  4 us
    ppermute x1, starting transfers between devices, body(): taper_in = lax.ppermute(given, 'bl', swap)  2.55 us
  transfers between devices with their start and end apart: 8, of which 4 were waited for; matrix products, arithmetic and copies ran while one was open for 0% of the time, Pallas kernels for 6%

profile of v3, /device:TPU:1, one launch (start us, length us, event | category | flops | bytes accessed | tf_op | source)
XLA Modules:
  0.0 107.3 jit_solution(5366836271944331891)
XLA Ops:
  0.0 1.1 %constant_dynamic-slice_fusion = f32[16,8192]{1,0:T(8,128)S(1)} fusion(f32[32,8192]{1,0:T(8,128)} %taper_own.1, s32[]{:T(128)S(6)} %select_n.9), kind=kLoop, calls=%fused_computation | loop fusion | bytes 1048580 | tf_op jit(solution)/shard_map/dynamic_slice | solution.py:373
  1.1 2.6 %collective-permute-start.3 = (f32[16,8192]{1,0:T(8,128)S(1)}, f32[16,8192]{1,0:T(8,128)S(1)}, u32[]{:S(2)}, u32[]{:S(2)}) collective-permute-start(f32[16,8192]{1,0:T(8,128)S(1)} %constant_dynamic-slice_fusion), channel_id=1, source_target_pairs={{0,128},{32,160},{64,192},{96,224},{128,0},{160,32},{192,64},{224,... | collective-permute-start | bytes 1572872 | tf_op jit(solution)/shard_map/ppermute | solution.py:374
  3.6 0.0 copy-start
  3.6 0.0 copy-start.7
  3.6 0.0 copy-start.8
  3.6 0.0 copy-start.9
  3.6 6.9 %shard_map.136 = (f32[33,8,128]{2,1,0:T(8,128)}, f32[33,8,128]{2,1,0:T(8,128)}, f32[33,8,128]{2,1,0:T(8,128)}, f32[33,8,128]{2,1,0:T(8,128)}, f32[33,8,128]{2,1,...) custom-call(s32[1]{0:T(128)} %bitcast.1.me, s32[1,8]{1,0:T(1,128)} %bitcast.14, ...), custom_call_target="tpu_custom_call" | custom-call | flops 4294967296 | bytes 8388608 | tf_op jit(solution)/shard_map/pallas_call | solution.py:160
  10.6 1.4 %collective-permute-start = (f32[33,8,128]{2,1,0:T(8,128)}, f32[33,8,128]{2,1,0:T(8,128)S(1)}, u32[]{:S(2)}, u32[]{:S(2)}) collective-permute-start(f32[33,8,128]{2,1,0:T(8,128)} %get-tuple-element.19), channel_id=1, source_target_pairs={{0,32},{32,0},{64,96},{96,64},{128,160},{160,128},{192,224},{224,1... | collective-permute-start | bytes 405512 | tf_op jit(solution)/shard_map/ppermute | solution.py:381
  11.9 2.6 %collective-permute-start.1 = (f32[33,8,128]{2,1,0:T(8,128)}, f32[33,8,128]{2,1,0:T(8,128)S(1)}, u32[]{:S(2)}, u32[]{:S(2)}) collective-permute-start(f32[33,8,128]{2,1,0:T(8,128)} %get-tuple-element.20), channel_id=1, source_target_pairs={{0,64},{32,96},{64,0},{96,32},{128,192},{160,224},{192,128},{224,1... | collective-permute-start | bytes 405512 | tf_op jit(solution)/shard_map/ppermute | solution.py:381
  14.6 0.0 collective-permute-start.2
  14.6 0.0 collective-permute-done.3.taper_in
  14.6 1.9 %collective-permute-start.4 = (f32[33,8,128]{2,1,0:T(8,128)}, f32[33,8,128]{2,1,0:T(8,128)S(1)}, u32[]{:S(2)}, u32[]{:S(2)}) collective-permute-start(f32[33,8,128]{2,1,0:T(8,128)} %get-tuple-element.26), channel_id=1, source_target_pairs={{0,128},{32,160},{64,192},{96,224},{128,0},{160,32},{192,64},{224,... | collective-permute-start | bytes 405512 | tf_op jit(solution)/shard_map/ppermute | solution.py:381
  16.4 1.2 %collective-permute-start.5 = (f32[33,8,128]{2,1,0:T(8,128)}, f32[33,8,128]{2,1,0:T(8,128)S(1)}, u32[]{:S(2)}, u32[]{:S(2)}) collective-permute-start(f32[33,8,128]{2,1,0:T(8,128)} %get-tuple-element.27), channel_id=1, source_target_pairs={{0,160},{32,128},{64,224},{96,192},{128,32},{160,0},{192,96},{224,... | collective-permute-start | bytes 405512 | tf_op jit(solution)/shard_map/ppermute | solution.py:381
  17.6 0.0 collective-permute-done.in1
  17.6 3.6 %collective-permute-start.6 = (f32[33,8,128]{2,1,0:T(8,128)}, f32[33,8,128]{2,1,0:T(8,128)S(1)}, u32[]{:S(2)}, u32[]{:S(2)}) collective-permute-start(f32[33,8,128]{2,1,0:T(8,128)} %get-tuple-element.28), channel_id=1, source_target_pairs={{0,192},{32,224},{64,128},{96,160},{128,64},{160,96},{192,0},{224,... | collective-permute-start | bytes 405512 | tf_op jit(solution)/shard_map/ppermute | solution.py:381
  21.2 0.0 collective-permute-done.1.in2
  21.2 0.0 collective-permute-start.7
  21.3 1.6 %collective-permute-done.2.in3 = f32[33,8,128]{2,1,0:T(8,128)S(1)} collective-permute-done((f32[33,8,128]{2,1,0:T(8,128)}, f32[33,8,128]{2,1,0:T(8,128)S(1)}, u32[]{:S(2)}, u32[]{:S(2)}) %collective-permute-start.2) | collective-permute-done | bytes 135200 | tf_op jit(solution)/shard_map/ppermute | solution.py:381
  22.9 0.0 collective-permute-done.4.in4
  22.9 0.2 collective-permute-done.5.in5
  23.0 5.5 %collective-permute-done.6.in6 = f32[33,8,128]{2,1,0:T(8,128)S(1)} collective-permute-done((f32[33,8,128]{2,1,0:T(8,128)}, f32[33,8,128]{2,1,0:T(8,128)S(1)}, u32[]{:S(2)}, u32[]{:S(2)}) %collective-permute-start.6) | collective-permute-done | bytes 135200 | tf_op jit(solution)/shard_map/ppermute | solution.py:381
  28.5 1.8 %collective-permute-done.7.in7 = f32[33,8,128]{2,1,0:T(8,128)S(1)} collective-permute-done((f32[33,8,128]{2,1,0:T(8,128)}, f32[33,8,128]{2,1,0:T(8,128)S(1)}, u32[]{:S(2)}, u32[]{:S(2)}) %collective-permute-start.7) | collective-permute-done | bytes 135200 | tf_op jit(solution)/shard_map/ppermute | solution.py:381
  30.2 0.0 copy-done
  30.2 0.0 copy-done.7
  30.2 0.0 copy-done.8
  30.3 0.0 copy-done.9
  30.3 0.0 copy-start.4
  30.3 0.9 copy-done.4
  31.2 4.0 %shard_map.137 = f32[2,128,16,128]{3,2,1,0:T(8,128)S(1)} custom-call(s32[1]{0:T(128)} %bitcast.side, f32[33,8,128]{2,1,0:T(8,128)S(1)} %copy-done.4, f32[33,8,128]{2,1,0:T(8,128)S(1)} %collective-permute-done.in1, f32[33,8,128]{2,1,0:T(8,128)S(1)} %collective-permute-done.1.in2, f32[33,8,128]{2,1,0:T(8,128)S(1)} %collective-permute-done.2.in3, ...), custom_call_target="tpu_custom_call" | custom-call | tf_op jit(solution)/shard_map/pallas_call | solution.py:263
  35.2 0.0 copy-start.1
  35.2 0.0 copy-start.2
  35.2 0.0 copy-start.3
  35.2 0.0 copy-start.5
  35.2 0.0 copy-start.6
  35.2 67.2 %all_to_all.5 = f32[256,16,128]{2,1,0:T(8,128)S(1)} all-to-all(f32[256,16,128]{2,1,0:T(8,128)S(1)} %bitcast.10), channel_id=1, replica_groups={{0,64,1,65,2,66,3,67,4,68,5,69,6,70,7,71,8,72,9,73,10,74,11,75,12,76,13..., dimensions={0} | all-to-all | bytes 4194304 | tf_op jit(solution)/shard_map/all_to_all | solution.py:386
  102.5 0.0 copy-done.1
  102.5 0.0 copy-done.2
  102.5 0.0 copy-done.3
  102.5 0.0 copy-done.5
  102.5 0.0 copy-done.6
  102.5 4.8 %shard_map.138 = f32[2,32,8192]{2,1,0:T(8,128)} custom-call(f32[4,64,16,128]{3,2,1,0:T(8,128)S(1)} %bitcast.9, bf16[256,256]{1,0:T(8,128)(2,1)S(1)} %copy-done.6, bf16[256,256]{1,0:T(8,128)(2,1)S(1)} %copy-done.5, f32[4,2,128,128]{3,2,1,0:T(8,128)S(1)} %copy-done.3, bf16[4,256,256]{2,1,0:T(8,128)(2,1)S(1)} %copy-done.2, bf16[4,256,256]{2,1,0:T(8,128)(2,1)S(1)} %copy-done.1), custom_call_target="tpu_custom_call" | custom-call | tf_op jit(solution)/shard_map/pallas_call | solution.py:353
Async XLA Ops:
  1.1 13.5 %collective-permute-start.3 = (f32[16,8192]{1,0:T(8,128)S(1)}, f32[16,8192]{1,0:T(8,128)S(1)}, u32[]{:S(2)}, u32[]{:S(2)}) collective-permute-start(f32[16,8192]{1,0:T(8,128)S(1)} %constant_dynamic-slice_fusion), channel_id=1, source_target_pairs={{0,128},{32,160},{64,192},{96,224},{128,0},{160,32},{192,64},{224,... | collective-permute-start | bytes 1572872 | tf_op jit(solution)/shard_map/ppermute | solution.py:374
  3.6 26.6 %copy-start = (f32[32,8192]{1,0:T(8,128)S(1)}, f32[32,8192]{1,0:T(8,128)}, u32[]{:S(2)}) copy-start(f32[32,8192]{1,0:T(8,128)} %taper_own.1) | copy-start | bytes 3145732
  3.6 26.6 %copy-start.7 = (bf16[256,256]{1,0:T(8,128)(2,1)S(1)}, bf16[256,256]{1,0:T(8,128)(2,1)}, u32[]{:S(2)}) copy-start(bf16[256,256]{1,0:T(8,128)(2,1)} %constant.46.clone.wl) | copy-start | bytes 393220
  3.6 26.6 %copy-start.8 = (bf16[256,256]{1,0:T(8,128)(2,1)S(1)}, bf16[256,256]{1,0:T(8,128)(2,1)}, u32[]{:S(2)}) copy-start(bf16[256,256]{1,0:T(8,128)(2,1)} %constant.45.clone.wh) | copy-start | bytes 393220
  3.6 26.6 %copy-start.9 = (f32[2,64,128]{2,1,0:T(8,128)S(1)}, f32[2,64,128]{2,1,0:T(8,128)}, u32[]{:S(2)}) copy-start(f32[2,64,128]{2,1,0:T(8,128)} %constant.44.clone.tw) | copy-start | bytes 196612
  10.6 7.1 %collective-permute-start = (f32[33,8,128]{2,1,0:T(8,128)}, f32[33,8,128]{2,1,0:T(8,128)S(1)}, u32[]{:S(2)}, u32[]{:S(2)}) collective-permute-start(f32[33,8,128]{2,1,0:T(8,128)} %get-tuple-element.19), channel_id=1, source_target_pairs={{0,32},{32,0},{64,96},{96,64},{128,160},{160,128},{192,224},{224,1... | collective-permute-start | bytes 405512 | tf_op jit(solution)/shard_map/ppermute | solution.py:381
  11.9 9.3 %collective-permute-start.1 = (f32[33,8,128]{2,1,0:T(8,128)}, f32[33,8,128]{2,1,0:T(8,128)S(1)}, u32[]{:S(2)}, u32[]{:S(2)}) collective-permute-start(f32[33,8,128]{2,1,0:T(8,128)} %get-tuple-element.20), channel_id=1, source_target_pairs={{0,64},{32,96},{64,0},{96,32},{128,192},{160,224},{192,128},{224,1... | collective-permute-start | bytes 405512 | tf_op jit(solution)/shard_map/ppermute | solution.py:381
  14.6 8.3 %collective-permute-start.2 = (f32[33,8,128]{2,1,0:T(8,128)}, f32[33,8,128]{2,1,0:T(8,128)S(1)}, u32[]{:S(2)}, u32[]{:S(2)}) collective-permute-start(f32[33,8,128]{2,1,0:T(8,128)} %get-tuple-element.21), channel_id=1, source_target_pairs={{0,96},{32,64},{64,32},{96,0},{128,224},{160,192},{192,160},{224,1... | collective-permute-start | bytes 405512 | tf_op jit(solution)/shard_map/ppermute | solution.py:381
  14.6 8.3 %collective-permute-start.4 = (f32[33,8,128]{2,1,0:T(8,128)}, f32[33,8,128]{2,1,0:T(8,128)S(1)}, u32[]{:S(2)}, u32[]{:S(2)}) collective-permute-start(f32[33,8,128]{2,1,0:T(8,128)} %get-tuple-element.26), channel_id=1, source_target_pairs={{0,128},{32,160},{64,192},{96,224},{128,0},{160,32},{192,64},{224,... | collective-permute-start | bytes 405512 | tf_op jit(solution)/shard_map/ppermute | solution.py:381
  16.4 6.6 %collective-permute-start.5 = (f32[33,8,128]{2,1,0:T(8,128)}, f32[33,8,128]{2,1,0:T(8,128)S(1)}, u32[]{:S(2)}, u32[]{:S(2)}) collective-permute-start(f32[33,8,128]{2,1,0:T(8,128)} %get-tuple-element.27), channel_id=1, source_target_pairs={{0,160},{32,128},{64,224},{96,192},{128,32},{160,0},{192,96},{224,... | collective-permute-start | bytes 405512 | tf_op jit(solution)/shard_map/ppermute | solution.py:381
  17.6 10.8 %collective-permute-start.6 = (f32[33,8,128]{2,1,0:T(8,128)}, f32[33,8,128]{2,1,0:T(8,128)S(1)}, u32[]{:S(2)}, u32[]{:S(2)}) collective-permute-start(f32[33,8,128]{2,1,0:T(8,128)} %get-tuple-element.28), channel_id=1, source_target_pairs={{0,192},{32,224},{64,128},{96,160},{128,64},{160,96},{192,0},{224,... | collective-permute-start | bytes 405512 | tf_op jit(solution)/shard_map/ppermute | solution.py:381
  21.2 9.0 %collective-permute-start.7 = (f32[33,8,128]{2,1,0:T(8,128)}, f32[33,8,128]{2,1,0:T(8,128)S(1)}, u32[]{:S(2)}, u32[]{:S(2)}) collective-permute-start(f32[33,8,128]{2,1,0:T(8,128)} %get-tuple-element.29), channel_id=1, source_target_pairs={{0,224},{32,192},{64,160},{96,128},{128,96},{160,64},{192,32},{224... | collective-permute-start | bytes 405512 | tf_op jit(solution)/shard_map/ppermute | solution.py:381
  30.3 0.9 copy-start.4
  35.2 67.3 %copy-start.1 = (bf16[4,256,256]{2,1,0:T(8,128)(2,1)S(1)}, bf16[4,256,256]{2,1,0:T(8,128)(2,1)}, u32[]{:S(2)}) copy-start(bf16[4,256,256]{2,1,0:T(8,128)(2,1)} %constant.51.clone.gl) | copy-start | bytes 1572868
  35.2 67.3 %copy-start.2 = (bf16[4,256,256]{2,1,0:T(8,128)(2,1)S(1)}, bf16[4,256,256]{2,1,0:T(8,128)(2,1)}, u32[]{:S(2)}) copy-start(bf16[4,256,256]{2,1,0:T(8,128)(2,1)} %constant.50.clone.gh) | copy-start | bytes 1572868
  35.2 67.3 %copy-start.3 = (f32[4,2,128,128]{3,2,1,0:T(8,128)S(1)}, f32[4,2,128,128]{3,2,1,0:T(8,128)}, u32[]{:S(2)}) copy-start(f32[4,2,128,128]{3,2,1,0:T(8,128)} %constant.49.clone.tw) | copy-start | bytes 1572868
  35.2 67.3 %copy-start.5 = (bf16[256,256]{1,0:T(8,128)(2,1)S(1)}, bf16[256,256]{1,0:T(8,128)(2,1)}, u32[]{:S(2)}) copy-start(bf16[256,256]{1,0:T(8,128)(2,1)} %constant.48.clone.w1l) | copy-start | bytes 393220
  35.2 67.3 %copy-start.6 = (bf16[256,256]{1,0:T(8,128)(2,1)S(1)}, bf16[256,256]{1,0:T(8,128)(2,1)}, u32[]{:S(2)}) copy-start(bf16[256,256]{1,0:T(8,128)(2,1)} %constant.47.clone.w1h) | copy-start | bytes 393220

commit v4 on v3

--- a/solution.py
+++ b/solution.py
@@ -133,8 +133,9 @@
         value, taken = rotated(s, 1)
         rights = split(value)
         right = jnp.concatenate([place(rights[h].astype(F32), taken) for h in range(2)], axis=0)
-        prod = lax.dot_general(left, right, NT, preferred_element_type=F32)
-        tile = (prod[:256, :128] + prod[256:, :128]) + (prod[:256, 128:] + prod[256:, 128:])
+        prod = lax.dot_general(left[:256], right, NT, preferred_element_type=F32)
+        tile = prod[:, :128] + prod[:, 128:]
+        tile += lax.dot_general(left[256:], right[:128], NT, preferred_element_type=F32)
         for p in range(2):
             for block in range(N_BL):
                 start = p * TILE + block * STRIP
@@ -161,7 +162,7 @@
         grid_kernel,
         out_shape=[jax.ShapeDtypeStruct((33, 8, TILE), F32)] * N_BL,
         in_specs=[pl.BlockSpec(memory_space=pltpu.SMEM)] + [hbm] * 5,
-        out_specs=[hbm] * N_BL,
+        out_specs=[pl.BlockSpec(memory_space=pltpu.VMEM)] + [hbm] * (N_BL - 1),
         scratch_shapes=[
             pltpu.SMEM((1, SLOTS), jnp.int32),
             pltpu.SMEM((1, SLOTS), jnp.int32),
@@ -179,8 +180,8 @@
 
 
 def column_kernel(
-    side, in_own, in1, in2, in3, in4, in5, in6, in7, taper_own, taper_in, tw, wh, wl, out,
-    taper, in0, cells, half, xh, xl, ob, number, place, sem_in,
+    side, in0, in1, in2, in3, in4, in5, in6, in7, taper_own, taper_in, tw, wh, wl, out,
+    taper, cells, half, xh, xl, ob, number, place, sem_in,
 ):
     mine = side[0]
     kept = pl.ds(pl.multiple_of(mine * STRIP, STRIP), STRIP)
@@ -188,23 +189,22 @@
     in_b = pltpu.make_async_copy(taper_in, taper.at[1 - mine], sem_in.at[1])
     in_a.start()
     in_b.start()
-    in_d = pltpu.make_async_copy(in_own, in0, sem_in.at[3])
-    in_d.start()
     strips = [in0, in1, in2, in3, in4, in5, in6, in7]
     for block in range(N_BL):
         rows = slice(block * SLOTS, (block + 1) * SLOTS)
-        if block == 0:
-            cells[...] = jnp.zeros_like(cells)
-            in_d.wait()
         number[rows, :] = strips[block][32].astype(jnp.int32)
     to_scalar = pltpu.make_async_copy(number, place, sem_in.at[2])
     to_scalar.start()
+    cells[...] = jnp.zeros_like(cells)
     to_scalar.wait()
 
     for block in range(N_BL):
-        for slot in range(SLOTS):
-            tile = place[block * SLOTS + slot, 0]
-            cells[tile] = cells[tile] + strips[block][slot * 4 : slot * 4 + 4]
+        tiles = [place[block * SLOTS + slot, 0] for slot in range(SLOTS)]
+        sums = [
+            cells[tile] + strips[block][slot * 4 : slot * 4 + 4] for slot, tile in enumerate(tiles)
+        ]
+        for tile, value in zip(tiles, sums):
+            cells[tile] = value
     in_a.wait()
     in_b.wait()
     for tr in range(BANDS):
@@ -263,11 +263,10 @@
     return pl.pallas_call(
         column_kernel,
         out_shape=jax.ShapeDtypeStruct((2, TILE, 16, TILE), F32),
-        in_specs=[smem, hbm] + [vmem] * (N_BL - 1) + [hbm, hbm, vmem, vmem, vmem],
+        in_specs=[smem] + [vmem] * N_BL + [hbm, hbm, vmem, vmem, vmem],
         out_specs=vmem,
         scratch_shapes=[
             pltpu.VMEM((2, STRIP, G), F32),
-            pltpu.VMEM((33, 8, TILE), F32),
             pltpu.VMEM((BANDS * COLS, 4, 8, TILE), F32),
             pltpu.VMEM((64, 32, TILE), F32),
             pltpu.VMEM((BANDS, 1024, 256), BF16),
@@ -275,13 +274,13 @@
             pltpu.VMEM((2, 2, 8, TILE, TILE), F32),
             pltpu.VMEM((64, TILE), jnp.int32),
             pltpu.SMEM((64, TILE), jnp.int32),
-            pltpu.SemaphoreType.DMA((4,)),
+            pltpu.SemaphoreType.DMA((3,)),
         ],
         compiler_params=pltpu.CompilerParams(vmem_limit_bytes=40 << 20),
     )(side, *strips, taper_own, taper_in, *column_tables())
 
 
-def row_kernel(arrived, w1h, w1l, tw, gh, gl, out, xh, xl, at, bh, bl):
+def row_kernel(arrived, w1h, w1l, tw, gh, gl, out, xh, xl, at, bh, bl, image, sem):
     for dl in range(4):
         for half in range(2):
             rows = jnp.swapaxes(arrived[dl, :, half * 8 : half * 8 + 8, :], 0, 1)
@@ -313,19 +312,29 @@
                 bl[kb, to_rows, p * TILE : (p + 1) * TILE] = low
         return carry
 
-    lax.fori_loop(0, 32, radix, 0)
-    for kb in range(4):
-        prod = lax.dot_general(gh[kb], bh[kb], NT, preferred_element_type=F32)
-        prod += lax.dot_general(gl[kb], bh[kb], NT, preferred_element_type=F32)
-        prod += lax.dot_general(gh[kb], bl[kb], NT, preferred_element_type=F32)
-        for p in range(2):
-            for k2 in range(16):
-                row = p * TILE + k2 * 8
-                to = (k2 * 4 + kb) * TILE
-                for mb in range(4):
-                    out[p, mb * 8 : mb * 8 + 8, to : to + TILE] = prod[
-                        row : row + 8, mb * TILE : (mb + 1) * TILE
-                    ]
+    lax.fori_loop(0, 32, radix, 0, unroll=4)
+    copies = []
+    for half in range(2):
+        rows = slice(half * 256, half * 256 + 256)
+        for kb in range(4):
+            prod = lax.dot_general(gh[kb], bh[kb, rows], NT, preferred_element_type=F32)
+            prod += lax.dot_general(gl[kb], bh[kb, rows], NT, preferred_element_type=F32)
+            prod += lax.dot_general(gh[kb], bl[kb, rows], NT, preferred_element_type=F32)
+            for p in range(2):
+                for k2 in range(16):
+                    row = p * TILE + k2 * 8
+                    to = (k2 * 4 + kb) * TILE
+                    for m in range(2):
+                        image[half, p, m * 8 : m * 8 + 8, to : to + TILE] = prod[
+                            row : row + 8, m * TILE : (m + 1) * TILE
+                        ]
+        copy = pltpu.make_async_copy(
+            image.at[half], out.at[:, pl.ds(half * 16, 16), :], sem.at[half]
+        )
+        copy.start()
+        copies.append(copy)
+    for copy in copies:
+        copy.wait()
 
 
 def row_tables():
@@ -354,13 +363,15 @@
         row_kernel,
         out_shape=jax.ShapeDtypeStruct((2, 32, G), F32),
         in_specs=[vmem, vmem, vmem, vmem, vmem, vmem],
-        out_specs=vmem,
+        out_specs=pl.BlockSpec(memory_space=HBM),
         scratch_shapes=[
             pltpu.VMEM((4, 256, 512), BF16),
             pltpu.VMEM((4, 256, 512), BF16),
             pltpu.VMEM((4, 256, 512), F32),
             pltpu.VMEM((4, 512, 256), BF16),
             pltpu.VMEM((4, 512, 256), BF16),
+            pltpu.VMEM((2, 2, 16, G), F32),
+            pltpu.SemaphoreType.DMA((2,)),
         ],
         compiler_params=pltpu.CompilerParams(vmem_limit_bytes=40 << 20),
     )(arrived, *row_tables())
@@ -375,8 +386,8 @@
     strips = grid_call(
         me.reshape(1).astype(jnp.int32), counts[0], slot_tiles[0], visibilities[0, 0], kernels[0, 0], offsets[0, 0]
     )
-    far, taper_in = lax.optimization_barrier((list(strips[4:]), taper_in))
-    blocks = list(strips[:4]) + far
+    far, taper_in = lax.optimization_barrier((list(strips[5:]), taper_in))
+    blocks = list(strips[:5]) + far
     strips = [blocks[0]] + [
         lax.ppermute(blocks[step], "bl", [(s, s ^ step) for s in range(N_BL)])
         for step in range(1, N_BL)

time: 108 us -> 105 us (0.972)
  Pallas kernels: 15.7 us -> 14.1 us
    ppermute x7, waiting for transfers between devices: 8.99 us -> 7.75 us  [body(): lax.ppermute(blocks[step], 'bl', [(s, s ^ step) for s in range(N_BL)])]
where the time goes in v4:
time: 105 us
  blocking collectives  67.6 us (64%)
  Pallas kernels  14.1 us (13%)
  starting transfers between devices  13.3 us (13%)
  waiting for transfers between devices  7.99 us (8%)
  local copies, waits for them, and re-layouts  2.03 us (2%)
    all_to_all x1, blocking collectives, body(): lax.all_to_all(leaving.reshape(256, 16, TILE), ('bl', 'row'), 0, 0, axis_...  67.6 us
    ppermute x7, starting transfers between devices, body(): lax.ppermute(blocks[step], 'bl', [(s, s ^ step) for s in range(N_BL)])  10.7 us
    ppermute x7, waiting for transfers between devices, body(): lax.ppermute(blocks[step], 'bl', [(s, s ^ step) for s in range(N_BL)])  7.75 us
    pallas_call x1, Pallas kernels, grid_call(): pl.pallas_call(grid_kernel, out_shape=[jax.ShapeDtypeStruct((33, 8, TILE)...  6.27 us
    pallas_call x1, Pallas kernels, row_call(): pl.pallas_call(row_kernel, out_shape=jax.ShapeDtypeStruct((2, 32, G), F32...  4.09 us
    pallas_call x1, Pallas kernels, column_call(): pl.pallas_call(column_kernel, out_shape=jax.ShapeDtypeStruct((2, TILE, 16...  3.72 us
    ppermute x1, starting transfers between devices, body(): taper_in = lax.ppermute(given, 'bl', swap)  2.55 us
  transfers between devices with their start and end apart: 8, of which 4 were waited for; matrix products, arithmetic and copies ran while one was open for 0% of the time, Pallas kernels for 6%

profile of v4, /device:TPU:1, one launch (start us, length us, event | category | flops | bytes accessed | tf_op | source)
XLA Modules:
  0.0 105.1 jit_solution(719928787713799404)
XLA Ops:
  0.0 1.1 %constant_dynamic-slice_fusion = f32[16,8192]{1,0:T(8,128)S(1)} fusion(f32[32,8192]{1,0:T(8,128)} %taper_own.1, s32[]{:T(128)S(6)} %select_n.9), kind=kLoop, calls=%fused_computation | loop fusion | bytes 1048580 | tf_op jit(solution)/shard_map/dynamic_slice | solution.py:384
  1.1 2.6 %collective-permute-start.4 = (f32[16,8192]{1,0:T(8,128)S(1)}, f32[16,8192]{1,0:T(8,128)S(1)}, u32[]{:S(2)}, u32[]{:S(2)}) collective-permute-start(f32[16,8192]{1,0:T(8,128)S(1)} %constant_dynamic-slice_fusion), channel_id=1, source_target_pairs={{0,128},{32,160},{64,192},{96,224},{128,0},{160,32},{192,64},{224,... | collective-permute-start | bytes 1572872 | tf_op jit(solution)/shard_map/ppermute | solution.py:385
  3.6 0.0 copy-start
  3.6 0.0 copy-start.7
  3.6 0.0 copy-start.8
  3.6 0.0 copy-start.9
  3.6 6.3 %shard_map.136 = (f32[33,8,128]{2,1,0:T(8,128)}, f32[33,8,128]{2,1,0:T(8,128)}, f32[33,8,128]{2,1,0:T(8,128)}, f32[33,8,128]{2,1,0:T(8,128)}, f32[33,8,128]{2,1,...) custom-call(s32[1]{0:T(128)} %bitcast.1.me, s32[1,8]{1,0:T(1,128)} %bitcast.14, ...), custom_call_target="tpu_custom_call" | custom-call | flops 4294967296 | bytes 8388608 | tf_op jit(solution)/shard_map/pallas_call | solution.py:161
  9.9 1.4 %collective-permute-start = (f32[33,8,128]{2,1,0:T(8,128)}, f32[33,8,128]{2,1,0:T(8,128)S(1)}, u32[]{:S(2)}, u32[]{:S(2)}) collective-permute-start(f32[33,8,128]{2,1,0:T(8,128)} %get-tuple-element.18), channel_id=1, source_target_pairs={{0,32},{32,0},{64,96},{96,64},{128,160},{160,128},{192,224},{224,1... | collective-permute-start | bytes 405512 | tf_op jit(solution)/shard_map/ppermute | solution.py:392
  11.3 2.6 %collective-permute-start.1 = (f32[33,8,128]{2,1,0:T(8,128)}, f32[33,8,128]{2,1,0:T(8,128)S(1)}, u32[]{:S(2)}, u32[]{:S(2)}) collective-permute-start(f32[33,8,128]{2,1,0:T(8,128)} %get-tuple-element.19), channel_id=1, source_target_pairs={{0,64},{32,96},{64,0},{96,32},{128,192},{160,224},{192,128},{224,1... | collective-permute-start | bytes 405512 | tf_op jit(solution)/shard_map/ppermute | solution.py:392
  13.9 0.0 collective-permute-start.2
  13.9 0.1 collective-permute-start.3
  14.0 0.2 collective-permute-done.4.taper_in
  14.2 3.2 %collective-permute-start.5 = (f32[33,8,128]{2,1,0:T(8,128)}, f32[33,8,128]{2,1,0:T(8,128)S(1)}, u32[]{:S(2)}, u32[]{:S(2)}) collective-permute-start(f32[33,8,128]{2,1,0:T(8,128)} %get-tuple-element.25), channel_id=1, source_target_pairs={{0,160},{32,128},{64,224},{96,192},{128,32},{160,0},{192,96},{224,... | collective-permute-start | bytes 405512 | tf_op jit(solution)/shard_map/ppermute | solution.py:392
  17.4 0.0 collective-permute-done.in1
  17.4 2.5 %collective-permute-start.6 = (f32[33,8,128]{2,1,0:T(8,128)}, f32[33,8,128]{2,1,0:T(8,128)S(1)}, u32[]{:S(2)}, u32[]{:S(2)}) collective-permute-start(f32[33,8,128]{2,1,0:T(8,128)} %get-tuple-element.26), channel_id=1, source_target_pairs={{0,192},{32,224},{64,128},{96,160},{128,64},{160,96},{192,0},{224,... | collective-permute-start | bytes 405512 | tf_op jit(solution)/shard_map/ppermute | solution.py:392
  20.0 0.0 collective-permute-done.1.in2
  20.0 0.9 collective-permute-start.7
  20.9 1.3 %collective-permute-done.2.in3 = f32[33,8,128]{2,1,0:T(8,128)S(1)} collective-permute-done((f32[33,8,128]{2,1,0:T(8,128)}, f32[33,8,128]{2,1,0:T(8,128)S(1)}, u32[]{:S(2)}, u32[]{:S(2)}) %collective-permute-start.2) | collective-permute-done | bytes 135200 | tf_op jit(solution)/shard_map/ppermute | solution.py:392
  22.2 0.0 collective-permute-done.3.in4
  22.2 0.0 collective-permute-done.5.in5
  22.2 3.7 %collective-permute-done.6.in6 = f32[33,8,128]{2,1,0:T(8,128)S(1)} collective-permute-done((f32[33,8,128]{2,1,0:T(8,128)}, f32[33,8,128]{2,1,0:T(8,128)S(1)}, u32[]{:S(2)}, u32[]{:S(2)}) %collective-permute-start.6) | collective-permute-done | bytes 135200 | tf_op jit(solution)/shard_map/ppermute | solution.py:392
  25.9 2.8 %collective-permute-done.7.in7 = f32[33,8,128]{2,1,0:T(8,128)S(1)} collective-permute-done((f32[33,8,128]{2,1,0:T(8,128)}, f32[33,8,128]{2,1,0:T(8,128)S(1)}, u32[]{:S(2)}, u32[]{:S(2)}) %collective-permute-start.7) | collective-permute-done | bytes 135200 | tf_op jit(solution)/shard_map/ppermute | solution.py:392
  28.7 0.0 copy-done
  28.7 0.0 copy-done.7
  28.7 0.0 copy-done.8
  28.7 0.0 copy-done.9
  28.7 0.0 copy-start.4
  28.7 0.9 copy-done.4
  29.6 3.7 %shard_map.137 = f32[2,128,16,128]{3,2,1,0:T(8,128)S(1)} custom-call(s32[1]{0:T(128)} %bitcast.side, f32[33,8,128]{2,1,0:T(8,128)S(1)} %copy-done.4, f32[33,8,128]{2,1,0:T(8,128)S(1)} %collective-permute-done.in1, f32[33,8,128]{2,1,0:T(8,128)S(1)} %collective-permute-done.1.in2, f32[33,8,128]{2,1,0:T(8,128)S(1)} %collective-permute-done.2.in3, ...), custom_call_target="tpu_custom_call" | custom-call | tf_op jit(solution)/shard_map/pallas_call | solution.py:263
  33.3 0.0 copy-start.1
  33.3 0.0 copy-start.2
  33.3 0.0 copy-start.3
  33.4 0.0 copy-start.5
  33.4 0.0 copy-start.6
  33.4 67.6 %all_to_all.5 = f32[256,16,128]{2,1,0:T(8,128)S(1)} all-to-all(f32[256,16,128]{2,1,0:T(8,128)S(1)} %bitcast.10), channel_id=1, replica_groups={{0,64,1,65,2,66,3,67,4,68,5,69,6,70,7,71,8,72,9,73,10,74,11,75,12,76,13..., dimensions={0} | all-to-all | bytes 4194304 | tf_op jit(solution)/shard_map/all_to_all | solution.py:397
  101.0 0.0 copy-done.1
  101.0 0.0 copy-done.2
  101.0 0.0 copy-done.3
  101.0 0.0 copy-done.5
  101.0 0.0 copy-done.6
  101.0 4.1 %shard_map.138 = f32[2,32,8192]{2,1,0:T(8,128)} custom-call(f32[4,64,16,128]{3,2,1,0:T(8,128)S(1)} %bitcast.9, bf16[256,256]{1,0:T(8,128)(2,1)S(1)} %copy-done.6, bf16[256,256]{1,0:T(8,128)(2,1)S(1)} %copy-done.5, f32[4,2,128,128]{3,2,1,0:T(8,128)S(1)} %copy-done.3, bf16[4,256,256]{2,1,0:T(8,128)(2,1)S(1)} %copy-done.2, bf16[4,256,256]{2,1,0:T(8,128)(2,1)S(1)} %copy-done.1), custom_call_target="tpu_custom_call" | custom-call | tf_op jit(solution)/shard_map/pallas_call | solution.py:362
Async XLA Ops:
  1.1 13.1 %collective-permute-start.4 = (f32[16,8192]{1,0:T(8,128)S(1)}, f32[16,8192]{1,0:T(8,128)S(1)}, u32[]{:S(2)}, u32[]{:S(2)}) collective-permute-start(f32[16,8192]{1,0:T(8,128)S(1)} %constant_dynamic-slice_fusion), channel_id=1, source_target_pairs={{0,128},{32,160},{64,192},{96,224},{128,0},{160,32},{192,64},{224,... | collective-permute-start | bytes 1572872 | tf_op jit(solution)/shard_map/ppermute | solution.py:385
  3.6 25.0 %copy-start = (f32[32,8192]{1,0:T(8,128)S(1)}, f32[32,8192]{1,0:T(8,128)}, u32[]{:S(2)}) copy-start(f32[32,8192]{1,0:T(8,128)} %taper_own.1) | copy-start | bytes 3145732
  3.6 25.0 %copy-start.7 = (bf16[256,256]{1,0:T(8,128)(2,1)S(1)}, bf16[256,256]{1,0:T(8,128)(2,1)}, u32[]{:S(2)}) copy-start(bf16[256,256]{1,0:T(8,128)(2,1)} %constant.46.clone.wl) | copy-start | bytes 393220
  3.6 25.0 %copy-start.8 = (bf16[256,256]{1,0:T(8,128)(2,1)S(1)}, bf16[256,256]{1,0:T(8,128)(2,1)}, u32[]{:S(2)}) copy-start(bf16[256,256]{1,0:T(8,128)(2,1)} %constant.45.clone.wh) | copy-start | bytes 393220
  3.6 25.0 %copy-start.9 = (f32[2,64,128]{2,1,0:T(8,128)S(1)}, f32[2,64,128]{2,1,0:T(8,128)}, u32[]{:S(2)}) copy-start(f32[2,64,128]{2,1,0:T(8,128)} %constant.44.clone.tw) | copy-start | bytes 196612
  9.9 7.5 %collective-permute-start = (f32[33,8,128]{2,1,0:T(8,128)}, f32[33,8,128]{2,1,0:T(8,128)S(1)}, u32[]{:S(2)}, u32[]{:S(2)}) collective-permute-start(f32[33,8,128]{2,1,0:T(8,128)} %get-tuple-element.18), channel_id=1, source_target_pairs={{0,32},{32,0},{64,96},{96,64},{128,160},{160,128},{192,224},{224,1... | collective-permute-start | bytes 405512 | tf_op jit(solution)/shard_map/ppermute | solution.py:392
  11.3 8.7 %collective-permute-start.1 = (f32[33,8,128]{2,1,0:T(8,128)}, f32[33,8,128]{2,1,0:T(8,128)S(1)}, u32[]{:S(2)}, u32[]{:S(2)}) collective-permute-start(f32[33,8,128]{2,1,0:T(8,128)} %get-tuple-element.19), channel_id=1, source_target_pairs={{0,64},{32,96},{64,0},{96,32},{128,192},{160,224},{192,128},{224,1... | collective-permute-start | bytes 405512 | tf_op jit(solution)/shard_map/ppermute | solution.py:392
  13.9 8.3 %collective-permute-start.2 = (f32[33,8,128]{2,1,0:T(8,128)}, f32[33,8,128]{2,1,0:T(8,128)S(1)}, u32[]{:S(2)}, u32[]{:S(2)}) collective-permute-start(f32[33,8,128]{2,1,0:T(8,128)} %get-tuple-element.20), channel_id=1, source_target_pairs={{0,96},{32,64},{64,32},{96,0},{128,224},{160,192},{192,160},{224,1... | collective-permute-start | bytes 405512 | tf_op jit(solution)/shard_map/ppermute | solution.py:392
  13.9 8.3 %collective-permute-start.3 = (f32[33,8,128]{2,1,0:T(8,128)}, f32[33,8,128]{2,1,0:T(8,128)S(1)}, u32[]{:S(2)}, u32[]{:S(2)}) collective-permute-start(f32[33,8,128]{2,1,0:T(8,128)} %get-tuple-element.21), channel_id=1, source_target_pairs={{0,128},{32,160},{64,192},{96,224},{128,0},{160,32},{192,64},{224,... | collective-permute-start | bytes 405512 | tf_op jit(solution)/shard_map/ppermute | solution.py:392
  14.2 8.0 %collective-permute-start.5 = (f32[33,8,128]{2,1,0:T(8,128)}, f32[33,8,128]{2,1,0:T(8,128)S(1)}, u32[]{:S(2)}, u32[]{:S(2)}) collective-permute-start(f32[33,8,128]{2,1,0:T(8,128)} %get-tuple-element.25), channel_id=1, source_target_pairs={{0,160},{32,128},{64,224},{96,192},{128,32},{160,0},{192,96},{224,... | collective-permute-start | bytes 405512 | tf_op jit(solution)/shard_map/ppermute | solution.py:392
  17.4 8.4 %collective-permute-start.6 = (f32[33,8,128]{2,1,0:T(8,128)}, f32[33,8,128]{2,1,0:T(8,128)S(1)}, u32[]{:S(2)}, u32[]{:S(2)}) collective-permute-start(f32[33,8,128]{2,1,0:T(8,128)} %get-tuple-element.26), channel_id=1, source_target_pairs={{0,192},{32,224},{64,128},{96,160},{128,64},{160,96},{192,0},{224,... | collective-permute-start | bytes 405512 | tf_op jit(solution)/shard_map/ppermute | solution.py:392
  20.0 8.7 %collective-permute-start.7 = (f32[33,8,128]{2,1,0:T(8,128)}, f32[33,8,128]{2,1,0:T(8,128)S(1)}, u32[]{:S(2)}, u32[]{:S(2)}) collective-permute-start(f32[33,8,128]{2,1,0:T(8,128)} %get-tuple-element.27), channel_id=1, source_target_pairs={{0,224},{32,192},{64,160},{96,128},{128,96},{160,64},{192,32},{224... | collective-permute-start | bytes 405512 | tf_op jit(solution)/shard_map/ppermute | solution.py:392
  28.7 0.9 copy-start.4
  33.3 67.7 %copy-start.1 = (bf16[4,256,256]{2,1,0:T(8,128)(2,1)S(1)}, bf16[4,256,256]{2,1,0:T(8,128)(2,1)}, u32[]{:S(2)}) copy-start(bf16[4,256,256]{2,1,0:T(8,128)(2,1)} %constant.51.clone.gl) | copy-start | bytes 1572868
  33.3 67.6 %copy-start.2 = (bf16[4,256,256]{2,1,0:T(8,128)(2,1)S(1)}, bf16[4,256,256]{2,1,0:T(8,128)(2,1)}, u32[]{:S(2)}) copy-start(bf16[4,256,256]{2,1,0:T(8,128)(2,1)} %constant.50.clone.gh) | copy-start | bytes 1572868
  33.3 67.6 %copy-start.3 = (f32[4,2,128,128]{3,2,1,0:T(8,128)S(1)}, f32[4,2,128,128]{3,2,1,0:T(8,128)}, u32[]{:S(2)}) copy-start(f32[4,2,128,128]{3,2,1,0:T(8,128)} %constant.49.clone.tw) | copy-start | bytes 1572868
  33.4 67.6 %copy-start.5 = (bf16[256,256]{1,0:T(8,128)(2,1)S(1)}, bf16[256,256]{1,0:T(8,128)(2,1)}, u32[]{:S(2)}) copy-start(bf16[256,256]{1,0:T(8,128)(2,1)} %constant.48.clone.w1l) | copy-start | bytes 393220
  33.4 67.6 %copy-start.6 = (bf16[256,256]{1,0:T(8,128)(2,1)S(1)}, bf16[256,256]{1,0:T(8,128)(2,1)}, u32[]{:S(2)}) copy-start(bf16[256,256]{1,0:T(8,128)(2,1)} %constant.47.clone.w1h) | copy-start | bytes 393220

commit v5 on v4

--- a/solution.py
+++ b/solution.py
@@ -18,6 +18,8 @@
 N_ROW = 32
 BANDS = 2
 STRIP = TILE // N_BL
+STEPS = (0, 1, 2, 3, 4, 5, 6, 7)
+FREE = 6
 COLS = G // TILE
 F32 = jnp.float32
 BF16 = jnp.bfloat16
@@ -144,7 +146,7 @@
         if s % 4 == 3:
             part = pl.ds(s // 4 * 16, 16 + s // 7)
             for step in range(N_BL):
-                other = me[0] ^ step
+                other = me[0] ^ STEPS[step]
                 copy = pltpu.make_async_copy(
                     strips.at[(other & 3) * 2 + (other >> 2), part],
                     outs[step].at[part],
@@ -386,11 +388,12 @@
     strips = grid_call(
         me.reshape(1).astype(jnp.int32), counts[0], slot_tiles[0], visibilities[0, 0], kernels[0, 0], offsets[0, 0]
     )
-    far, taper_in = lax.optimization_barrier((list(strips[5:]), taper_in))
-    blocks = list(strips[:5]) + far
-    strips = [blocks[0]] + [
-        lax.ppermute(blocks[step], "bl", [(s, s ^ step) for s in range(N_BL)])
-        for step in range(1, N_BL)
+    far, taper_in = lax.optimization_barrier((list(strips[FREE:]), taper_in))
+    blocks = list(strips[:FREE]) + list(far)
+    own = blocks[0] + 0.0 * me.astype(F32)
+    strips = [own] + [
+        lax.ppermute(blocks[i], "bl", [(s, s ^ STEPS[i]) for s in range(N_BL)])
+        for i in range(1, N_BL)
     ]
     side = side.reshape(1).astype(jnp.int32)
     leaving = column_call(side, strips, taper, taper_in)

time: 105 us -> 104 us (level)
  transfers between devices with their start and end apart: 8 -> 8, of which waited for: 4 -> 4; matrix products, arithmetic and copies ran while one was open for 0% -> 1% of each run, Pallas kernels for 6% -> 6%
where the time goes in v5:
time: 104 us
  blocking collectives  67.6 us (65%)
  Pallas kernels  14.1 us (14%)
  starting transfers between devices  13.3 us (13%)
  waiting for transfers between devices  7.1 us (7%)
  local copies, waits for them, and re-layouts  1.12 us (1%)
    all_to_all x1, blocking collectives, body(): lax.all_to_all(leaving.reshape(256, 16, TILE), ('bl', 'row'), 0, 0, axis_...  67.6 us
    ppermute x7, starting transfers between devices, body(): lax.ppermute(blocks[i], 'bl', [(s, s ^ STEPS[i]) for s in range(N_BL)])  10.7 us
    ppermute x7, waiting for transfers between devices, body(): lax.ppermute(blocks[i], 'bl', [(s, s ^ STEPS[i]) for s in range(N_BL)])  6.84 us
    pallas_call x1, Pallas kernels, grid_call(): pl.pallas_call(grid_kernel, out_shape=[jax.ShapeDtypeStruct((33, 8, TILE)...  6.26 us
    pallas_call x1, Pallas kernels, row_call(): pl.pallas_call(row_kernel, out_shape=jax.ShapeDtypeStruct((2, 32, G), F32...  4.09 us
    pallas_call x1, Pallas kernels, column_call(): pl.pallas_call(column_kernel, out_shape=jax.ShapeDtypeStruct((2, TILE, 16...  3.73 us
    ppermute x1, starting transfers between devices, body(): taper_in = lax.ppermute(given, 'bl', swap)  2.55 us
  transfers between devices with their start and end apart: 8, of which 4 were waited for; matrix products, arithmetic and copies ran while one was open for 1% of the time, Pallas kernels for 6%

profile of v5, /device:TPU:1, one launch (start us, length us, event | category | flops | bytes accessed | tf_op | source)
XLA Modules:
  0.0 104.2 jit_solution(14162273491921163636)
XLA Ops:
  0.0 1.1 %constant_dynamic-slice_fusion = f32[16,8192]{1,0:T(8,128)S(1)} fusion(f32[32,8192]{1,0:T(8,128)} %taper_own.1, s32[]{:T(128)S(6)} %select_n.9), kind=kLoop, calls=%fused_computation.1 | loop fusion | bytes 1048580 | tf_op jit(solution)/shard_map/dynamic_slice | solution.py:386
  1.1 2.6 %collective-permute-start.5 = (f32[16,8192]{1,0:T(8,128)S(1)}, f32[16,8192]{1,0:T(8,128)S(1)}, u32[]{:S(2)}, u32[]{:S(2)}) collective-permute-start(f32[16,8192]{1,0:T(8,128)S(1)} %constant_dynamic-slice_fusion), channel_id=1, source_target_pairs={{0,128},{32,160},{64,192},{96,224},{128,0},{160,32},{192,64},{224,... | collective-permute-start | bytes 1572872 | tf_op jit(solution)/shard_map/ppermute | solution.py:387
  3.6 0.0 copy-start
  3.6 0.0 copy-start.6
  3.6 0.0 copy-start.7
  3.6 0.0 copy-start.8
  3.6 6.3 %shard_map.136 = (f32[33,8,128]{2,1,0:T(8,128)}, f32[33,8,128]{2,1,0:T(8,128)}, f32[33,8,128]{2,1,0:T(8,128)}, f32[33,8,128]{2,1,0:T(8,128)}, f32[33,8,128]{2,1,...) custom-call(s32[1]{0:T(128)} %bitcast.1.me, s32[1,8]{1,0:T(1,128)} %bitcast.14, ...), custom_call_target="tpu_custom_call" | custom-call | flops 4294967296 | bytes 8388608 | tf_op jit(solution)/shard_map/pallas_call | solution.py:163
  9.9 1.4 %collective-permute-start = (f32[33,8,128]{2,1,0:T(8,128)}, f32[33,8,128]{2,1,0:T(8,128)S(1)}, u32[]{:S(2)}, u32[]{:S(2)}) collective-permute-start(f32[33,8,128]{2,1,0:T(8,128)} %get-tuple-element.17), channel_id=1, source_target_pairs={{0,32},{32,0},{64,96},{96,64},{128,160},{160,128},{192,224},{224,1... | collective-permute-start | bytes 405512 | tf_op jit(solution)/shard_map/ppermute | solution.py:395
  11.3 2.6 %collective-permute-start.1 = (f32[33,8,128]{2,1,0:T(8,128)}, f32[33,8,128]{2,1,0:T(8,128)S(1)}, u32[]{:S(2)}, u32[]{:S(2)}) collective-permute-start(f32[33,8,128]{2,1,0:T(8,128)} %get-tuple-element.18), channel_id=1, source_target_pairs={{0,64},{32,96},{64,0},{96,32},{128,192},{160,224},{192,128},{224,1... | collective-permute-start | bytes 405512 | tf_op jit(solution)/shard_map/ppermute | solution.py:395
  13.9 0.0 collective-permute-start.2
  13.9 0.1 collective-permute-start.3
  14.0 0.3 collective-permute-done.5.taper_in
  14.2 3.2 %collective-permute-start.4 = (f32[33,8,128]{2,1,0:T(8,128)}, f32[33,8,128]{2,1,0:T(8,128)S(1)}, u32[]{:S(2)}, u32[]{:S(2)}) collective-permute-start(f32[33,8,128]{2,1,0:T(8,128)} %get-tuple-element.21), channel_id=1, source_target_pairs={{0,160},{32,128},{64,224},{96,192},{128,32},{160,0},{192,96},{224,... | collective-permute-start | bytes 405512 | tf_op jit(solution)/shard_map/ppermute | solution.py:395
  17.4 0.0 collective-permute-done.in1
  17.4 2.5 %collective-permute-start.6 = (f32[33,8,128]{2,1,0:T(8,128)}, f32[33,8,128]{2,1,0:T(8,128)S(1)}, u32[]{:S(2)}, u32[]{:S(2)}) collective-permute-start(f32[33,8,128]{2,1,0:T(8,128)} %get-tuple-element.24), channel_id=1, source_target_pairs={{0,192},{32,224},{64,128},{96,160},{128,64},{160,96},{192,0},{224,... | collective-permute-start | bytes 405512 | tf_op jit(solution)/shard_map/ppermute | solution.py:395
  20.0 0.0 collective-permute-done.1.in2
  20.0 0.9 collective-permute-start.7
  20.9 0.9 broadcast_add_fusion.in0
  21.8 0.4 collective-permute-done.2.in3
  22.2 0.0 collective-permute-done.3.in4
  22.2 0.0 collective-permute-done.4.in5
  22.2 3.6 %collective-permute-done.6.in6 = f32[33,8,128]{2,1,0:T(8,128)S(1)} collective-permute-done((f32[33,8,128]{2,1,0:T(8,128)}, f32[33,8,128]{2,1,0:T(8,128)S(1)}, u32[]{:S(2)}, u32[]{:S(2)}) %collective-permute-start.6) | collective-permute-done | bytes 135200 | tf_op jit(solution)/shard_map/ppermute | solution.py:395
  25.9 2.8 %collective-permute-done.7.in7 = f32[33,8,128]{2,1,0:T(8,128)S(1)} collective-permute-done((f32[33,8,128]{2,1,0:T(8,128)}, f32[33,8,128]{2,1,0:T(8,128)S(1)}, u32[]{:S(2)}, u32[]{:S(2)}) %collective-permute-start.7) | collective-permute-done | bytes 135200 | tf_op jit(solution)/shard_map/ppermute | solution.py:395
  28.7 0.0 copy-done
  28.7 0.0 copy-done.6
  28.7 0.0 copy-done.7
  28.7 0.0 copy-done.8
  28.7 3.7 %shard_map.137 = f32[2,128,16,128]{3,2,1,0:T(8,128)S(1)} custom-call(s32[1]{0:T(128)} %bitcast.side, f32[33,8,128]{2,1,0:T(8,128)S(1)} %broadcast_add_fusion.in0, f32[33,8,128]{2,1,0:T(8,128)S(1)} %collective-permute-done.in1, f32[33,8,128]{2,1,0:T(8,128)S(1)} %collective-permute-done.1.in2, f32[33,8,128]{2,1,0:T(8,128)S(1)} %collective-permute-done.2.in3, ...), custom_call_target="tpu_custom_call" | custom-call | tf_op jit(solution)/shard_map/pallas_call | solution.py:265
  32.4 0.0 copy-start.1
  32.4 0.0 copy-start.2
  32.4 0.0 copy-start.3
  32.5 0.0 copy-start.4
  32.5 0.0 copy-start.5
  32.5 67.6 %all_to_all.5 = f32[256,16,128]{2,1,0:T(8,128)S(1)} all-to-all(f32[256,16,128]{2,1,0:T(8,128)S(1)} %bitcast.10), channel_id=1, replica_groups={{0,64,1,65,2,66,3,67,4,68,5,69,6,70,7,71,8,72,9,73,10,74,11,75,12,76,13..., dimensions={0} | all-to-all | bytes 4194304 | tf_op jit(solution)/shard_map/all_to_all | solution.py:400
  100.1 0.0 copy-done.1
  100.1 0.0 copy-done.2
  100.1 0.0 copy-done.3
  100.1 0.0 copy-done.4
  100.1 0.0 copy-done.5
  100.1 4.1 %shard_map.138 = f32[2,32,8192]{2,1,0:T(8,128)} custom-call(f32[4,64,16,128]{3,2,1,0:T(8,128)S(1)} %bitcast.9, bf16[256,256]{1,0:T(8,128)(2,1)S(1)} %copy-done.5, bf16[256,256]{1,0:T(8,128)(2,1)S(1)} %copy-done.4, f32[4,2,128,128]{3,2,1,0:T(8,128)S(1)} %copy-done.3, bf16[4,256,256]{2,1,0:T(8,128)(2,1)S(1)} %copy-done.2, bf16[4,256,256]{2,1,0:T(8,128)(2,1)S(1)} %copy-done.1), custom_call_target="tpu_custom_call" | custom-call | tf_op jit(solution)/shard_map/pallas_call | solution.py:364
Async XLA Ops:
  1.1 13.1 %collective-permute-start.5 = (f32[16,8192]{1,0:T(8,128)S(1)}, f32[16,8192]{1,0:T(8,128)S(1)}, u32[]{:S(2)}, u32[]{:S(2)}) collective-permute-start(f32[16,8192]{1,0:T(8,128)S(1)} %constant_dynamic-slice_fusion), channel_id=1, source_target_pairs={{0,128},{32,160},{64,192},{96,224},{128,0},{160,32},{192,64},{224,... | collective-permute-start | bytes 1572872 | tf_op jit(solution)/shard_map/ppermute | solution.py:387
  3.6 25.0 %copy-start = (f32[32,8192]{1,0:T(8,128)S(1)}, f32[32,8192]{1,0:T(8,128)}, u32[]{:S(2)}) copy-start(f32[32,8192]{1,0:T(8,128)} %taper_own.1) | copy-start | bytes 3145732
  3.6 25.0 %copy-start.6 = (bf16[256,256]{1,0:T(8,128)(2,1)S(1)}, bf16[256,256]{1,0:T(8,128)(2,1)}, u32[]{:S(2)}) copy-start(bf16[256,256]{1,0:T(8,128)(2,1)} %constant.48.clone.wl) | copy-start | bytes 393220
  3.6 25.0 %copy-start.7 = (bf16[256,256]{1,0:T(8,128)(2,1)S(1)}, bf16[256,256]{1,0:T(8,128)(2,1)}, u32[]{:S(2)}) copy-start(bf16[256,256]{1,0:T(8,128)(2,1)} %constant.47.clone.wh) | copy-start | bytes 393220
  3.6 25.0 %copy-start.8 = (f32[2,64,128]{2,1,0:T(8,128)S(1)}, f32[2,64,128]{2,1,0:T(8,128)}, u32[]{:S(2)}) copy-start(f32[2,64,128]{2,1,0:T(8,128)} %constant.46.clone.tw) | copy-start | bytes 196612
  9.9 7.5 %collective-permute-start = (f32[33,8,128]{2,1,0:T(8,128)}, f32[33,8,128]{2,1,0:T(8,128)S(1)}, u32[]{:S(2)}, u32[]{:S(2)}) collective-permute-start(f32[33,8,128]{2,1,0:T(8,128)} %get-tuple-element.17), channel_id=1, source_target_pairs={{0,32},{32,0},{64,96},{96,64},{128,160},{160,128},{192,224},{224,1... | collective-permute-start | bytes 405512 | tf_op jit(solution)/shard_map/ppermute | solution.py:395
  11.3 8.7 %collective-permute-start.1 = (f32[33,8,128]{2,1,0:T(8,128)}, f32[33,8,128]{2,1,0:T(8,128)S(1)}, u32[]{:S(2)}, u32[]{:S(2)}) collective-permute-start(f32[33,8,128]{2,1,0:T(8,128)} %get-tuple-element.18), channel_id=1, source_target_pairs={{0,64},{32,96},{64,0},{96,32},{128,192},{160,224},{192,128},{224,1... | collective-permute-start | bytes 405512 | tf_op jit(solution)/shard_map/ppermute | solution.py:395
  13.9 8.3 %collective-permute-start.2 = (f32[33,8,128]{2,1,0:T(8,128)}, f32[33,8,128]{2,1,0:T(8,128)S(1)}, u32[]{:S(2)}, u32[]{:S(2)}) collective-permute-start(f32[33,8,128]{2,1,0:T(8,128)} %get-tuple-element.19), channel_id=1, source_target_pairs={{0,96},{32,64},{64,32},{96,0},{128,224},{160,192},{192,160},{224,1... | collective-permute-start | bytes 405512 | tf_op jit(solution)/shard_map/ppermute | solution.py:395
  13.9 8.3 %collective-permute-start.3 = (f32[33,8,128]{2,1,0:T(8,128)}, f32[33,8,128]{2,1,0:T(8,128)S(1)}, u32[]{:S(2)}, u32[]{:S(2)}) collective-permute-start(f32[33,8,128]{2,1,0:T(8,128)} %get-tuple-element.20), channel_id=1, source_target_pairs={{0,128},{32,160},{64,192},{96,224},{128,0},{160,32},{192,64},{224,... | collective-permute-start | bytes 405512 | tf_op jit(solution)/shard_map/ppermute | solution.py:395
  14.2 8.0 %collective-permute-start.4 = (f32[33,8,128]{2,1,0:T(8,128)}, f32[33,8,128]{2,1,0:T(8,128)S(1)}, u32[]{:S(2)}, u32[]{:S(2)}) collective-permute-start(f32[33,8,128]{2,1,0:T(8,128)} %get-tuple-element.21), channel_id=1, source_target_pairs={{0,160},{32,128},{64,224},{96,192},{128,32},{160,0},{192,96},{224,... | collective-permute-start | bytes 405512 | tf_op jit(solution)/shard_map/ppermute | solution.py:395
  17.4 8.4 %collective-permute-start.6 = (f32[33,8,128]{2,1,0:T(8,128)}, f32[33,8,128]{2,1,0:T(8,128)S(1)}, u32[]{:S(2)}, u32[]{:S(2)}) collective-permute-start(f32[33,8,128]{2,1,0:T(8,128)} %get-tuple-element.24), channel_id=1, source_target_pairs={{0,192},{32,224},{64,128},{96,160},{128,64},{160,96},{192,0},{224,... | collective-permute-start | bytes 405512 | tf_op jit(solution)/shard_map/ppermute | solution.py:395
  20.0 8.7 %collective-permute-start.7 = (f32[33,8,128]{2,1,0:T(8,128)}, f32[33,8,128]{2,1,0:T(8,128)S(1)}, u32[]{:S(2)}, u32[]{:S(2)}) collective-permute-start(f32[33,8,128]{2,1,0:T(8,128)} %get-tuple-element.25), channel_id=1, source_target_pairs={{0,224},{32,192},{64,160},{96,128},{128,96},{160,64},{192,32},{224... | collective-permute-start | bytes 405512 | tf_op jit(solution)/shard_map/ppermute | solution.py:395
  32.4 67.7 %copy-start.1 = (bf16[4,256,256]{2,1,0:T(8,128)(2,1)S(1)}, bf16[4,256,256]{2,1,0:T(8,128)(2,1)}, u32[]{:S(2)}) copy-start(bf16[4,256,256]{2,1,0:T(8,128)(2,1)} %constant.53.clone.gl) | copy-start | bytes 1572868
  32.4 67.6 %copy-start.2 = (bf16[4,256,256]{2,1,0:T(8,128)(2,1)S(1)}, bf16[4,256,256]{2,1,0:T(8,128)(2,1)}, u32[]{:S(2)}) copy-start(bf16[4,256,256]{2,1,0:T(8,128)(2,1)} %constant.52.clone.gh) | copy-start | bytes 1572868
  32.4 67.6 %copy-start.3 = (f32[4,2,128,128]{3,2,1,0:T(8,128)S(1)}, f32[4,2,128,128]{3,2,1,0:T(8,128)}, u32[]{:S(2)}) copy-start(f32[4,2,128,128]{3,2,1,0:T(8,128)} %constant.51.clone.tw) | copy-start | bytes 1572868
  32.5 67.6 %copy-start.4 = (bf16[256,256]{1,0:T(8,128)(2,1)S(1)}, bf16[256,256]{1,0:T(8,128)(2,1)}, u32[]{:S(2)}) copy-start(bf16[256,256]{1,0:T(8,128)(2,1)} %constant.50.clone.w1l) | copy-start | bytes 393220
  32.5 67.6 %copy-start.5 = (bf16[256,256]{1,0:T(8,128)(2,1)S(1)}, bf16[256,256]{1,0:T(8,128)(2,1)}, u32[]{:S(2)}) copy-start(bf16[256,256]{1,0:T(8,128)(2,1)} %constant.49.clone.w1h) | copy-start | bytes 393220

commit v6 on v5

--- a/solution.py
+++ b/solution.py
@@ -314,9 +314,9 @@
                 bl[kb, to_rows, p * TILE : (p + 1) * TILE] = low
         return carry
 
-    lax.fori_loop(0, 32, radix, 0, unroll=4)
     copies = []
     for half in range(2):
+        lax.fori_loop(half * 16, half * 16 + 16, radix, 0, unroll=8)
         rows = slice(half * 256, half * 256 + 256)
         for kb in range(4):
             prod = lax.dot_general(gh[kb], bh[kb, rows], NT, preferred_element_type=F32)

time: 104 us -> 105 us (level)
  no operation moved by 1% of the time
where the time goes in v6:
time: 105 us; the launch traced here: 104 us
  blocking collectives  67.6 us (64%)
  Pallas kernels  14.3 us (14%)
  starting transfers between devices  13.3 us (13%)
  waiting for transfers between devices  7.1 us (7%)
  local copies, waits for them, and re-layouts  1.12 us (1%)
    all_to_all x1, blocking collectives, body(): lax.all_to_all(leaving.reshape(256, 16, TILE), ('bl', 'row'), 0, 0, axis_...  67.6 us
    ppermute x7, starting transfers between devices, body(): lax.ppermute(blocks[i], 'bl', [(s, s ^ STEPS[i]) for s in range(N_BL)])  10.7 us
    ppermute x7, waiting for transfers between devices, body(): lax.ppermute(blocks[i], 'bl', [(s, s ^ STEPS[i]) for s in range(N_BL)])  6.84 us
    pallas_call x1, Pallas kernels, grid_call(): pl.pallas_call(grid_kernel, out_shape=[jax.ShapeDtypeStruct((33, 8, TILE)...  6.26 us
    pallas_call x1, Pallas kernels, row_call(): pl.pallas_call(row_kernel, out_shape=jax.ShapeDtypeStruct((2, 32, G), F32...  4.31 us
    pallas_call x1, Pallas kernels, column_call(): pl.pallas_call(column_kernel, out_shape=jax.ShapeDtypeStruct((2, TILE, 16...  3.73 us
    ppermute x1, starting transfers between devices, body(): taper_in = lax.ppermute(given, 'bl', swap)  2.55 us
  transfers between devices with their start and end apart: 8, of which 4 were waited for; matrix products, arithmetic and copies ran while one was open for 1% of the time, Pallas kernels for 6%

profile of v6, /device:TPU:1, one launch (start us, length us, event | category | flops | bytes accessed | tf_op | source)
XLA Modules:
  0.0 104.4 jit_solution(18404581412663352374)
XLA Ops:
  0.0 1.1 %constant_dynamic-slice_fusion = f32[16,8192]{1,0:T(8,128)S(1)} fusion(f32[32,8192]{1,0:T(8,128)} %taper_own.1, s32[]{:T(128)S(6)} %select_n.9), kind=kLoop, calls=%fused_computation.1 | loop fusion | bytes 1048580 | tf_op jit(solution)/shard_map/dynamic_slice | solution.py:386
  1.1 2.6 %collective-permute-start.5 = (f32[16,8192]{1,0:T(8,128)S(1)}, f32[16,8192]{1,0:T(8,128)S(1)}, u32[]{:S(2)}, u32[]{:S(2)}) collective-permute-start(f32[16,8192]{1,0:T(8,128)S(1)} %constant_dynamic-slice_fusion), channel_id=1, source_target_pairs={{0,128},{32,160},{64,192},{96,224},{128,0},{160,32},{192,64},{224,... | collective-permute-start | bytes 1572872 | tf_op jit(solution)/shard_map/ppermute | solution.py:387
  3.6 0.0 copy-start
  3.6 0.0 copy-start.6
  3.6 0.0 copy-start.7
  3.6 0.0 copy-start.8
  3.6 6.3 %shard_map.136 = (f32[33,8,128]{2,1,0:T(8,128)}, f32[33,8,128]{2,1,0:T(8,128)}, f32[33,8,128]{2,1,0:T(8,128)}, f32[33,8,128]{2,1,0:T(8,128)}, f32[33,8,128]{2,1,...) custom-call(s32[1]{0:T(128)} %bitcast.1.me, s32[1,8]{1,0:T(1,128)} %bitcast.14, ...), custom_call_target="tpu_custom_call" | custom-call | flops 4294967296 | bytes 8388608 | tf_op jit(solution)/shard_map/pallas_call | solution.py:163
  9.9 1.4 %collective-permute-start = (f32[33,8,128]{2,1,0:T(8,128)}, f32[33,8,128]{2,1,0:T(8,128)S(1)}, u32[]{:S(2)}, u32[]{:S(2)}) collective-permute-start(f32[33,8,128]{2,1,0:T(8,128)} %get-tuple-element.17), channel_id=1, source_target_pairs={{0,32},{32,0},{64,96},{96,64},{128,160},{160,128},{192,224},{224,1... | collective-permute-start | bytes 405512 | tf_op jit(solution)/shard_map/ppermute | solution.py:395
  11.3 2.6 %collective-permute-start.1 = (f32[33,8,128]{2,1,0:T(8,128)}, f32[33,8,128]{2,1,0:T(8,128)S(1)}, u32[]{:S(2)}, u32[]{:S(2)}) collective-permute-start(f32[33,8,128]{2,1,0:T(8,128)} %get-tuple-element.18), channel_id=1, source_target_pairs={{0,64},{32,96},{64,0},{96,32},{128,192},{160,224},{192,128},{224,1... | collective-permute-start | bytes 405512 | tf_op jit(solution)/shard_map/ppermute | solution.py:395
  13.9 0.0 collective-permute-start.2
  13.9 0.1 collective-permute-start.3
  14.0 0.3 collective-permute-done.5.taper_in
  14.2 3.2 %collective-permute-start.4 = (f32[33,8,128]{2,1,0:T(8,128)}, f32[33,8,128]{2,1,0:T(8,128)S(1)}, u32[]{:S(2)}, u32[]{:S(2)}) collective-permute-start(f32[33,8,128]{2,1,0:T(8,128)} %get-tuple-element.21), channel_id=1, source_target_pairs={{0,160},{32,128},{64,224},{96,192},{128,32},{160,0},{192,96},{224,... | collective-permute-start | bytes 405512 | tf_op jit(solution)/shard_map/ppermute | solution.py:395
  17.4 0.0 collective-permute-done.in1
  17.4 2.5 %collective-permute-start.6 = (f32[33,8,128]{2,1,0:T(8,128)}, f32[33,8,128]{2,1,0:T(8,128)S(1)}, u32[]{:S(2)}, u32[]{:S(2)}) collective-permute-start(f32[33,8,128]{2,1,0:T(8,128)} %get-tuple-element.24), channel_id=1, source_target_pairs={{0,192},{32,224},{64,128},{96,160},{128,64},{160,96},{192,0},{224,... | collective-permute-start | bytes 405512 | tf_op jit(solution)/shard_map/ppermute | solution.py:395
  20.0 0.0 collective-permute-done.1.in2
  20.0 0.9 collective-permute-start.7
  20.9 0.9 broadcast_add_fusion.in0
  21.8 0.4 collective-permute-done.2.in3
  22.2 0.0 collective-permute-done.3.in4
  22.2 0.0 collective-permute-done.4.in5
  22.2 3.6 %collective-permute-done.6.in6 = f32[33,8,128]{2,1,0:T(8,128)S(1)} collective-permute-done((f32[33,8,128]{2,1,0:T(8,128)}, f32[33,8,128]{2,1,0:T(8,128)S(1)}, u32[]{:S(2)}, u32[]{:S(2)}) %collective-permute-start.6) | collective-permute-done | bytes 135200 | tf_op jit(solution)/shard_map/ppermute | solution.py:395
  25.9 2.8 %collective-permute-done.7.in7 = f32[33,8,128]{2,1,0:T(8,128)S(1)} collective-permute-done((f32[33,8,128]{2,1,0:T(8,128)}, f32[33,8,128]{2,1,0:T(8,128)S(1)}, u32[]{:S(2)}, u32[]{:S(2)}) %collective-permute-start.7) | collective-permute-done | bytes 135200 | tf_op jit(solution)/shard_map/ppermute | solution.py:395
  28.7 0.0 copy-done
  28.7 0.0 copy-done.6
  28.7 0.0 copy-done.7
  28.7 0.0 copy-done.8
  28.7 3.7 %shard_map.137 = f32[2,128,16,128]{3,2,1,0:T(8,128)S(1)} custom-call(s32[1]{0:T(128)} %bitcast.side, f32[33,8,128]{2,1,0:T(8,128)S(1)} %broadcast_add_fusion.in0, f32[33,8,128]{2,1,0:T(8,128)S(1)} %collective-permute-done.in1, f32[33,8,128]{2,1,0:T(8,128)S(1)} %collective-permute-done.1.in2, f32[33,8,128]{2,1,0:T(8,128)S(1)} %collective-permute-done.2.in3, ...), custom_call_target="tpu_custom_call" | custom-call | tf_op jit(solution)/shard_map/pallas_call | solution.py:265
  32.4 0.0 copy-start.1
  32.4 0.0 copy-start.2
  32.4 0.0 copy-start.3
  32.5 0.0 copy-start.4
  32.5 0.0 copy-start.5
  32.5 67.6 %all_to_all.5 = f32[256,16,128]{2,1,0:T(8,128)S(1)} all-to-all(f32[256,16,128]{2,1,0:T(8,128)S(1)} %bitcast.10), channel_id=1, replica_groups={{0,64,1,65,2,66,3,67,4,68,5,69,6,70,7,71,8,72,9,73,10,74,11,75,12,76,13..., dimensions={0} | all-to-all | bytes 4194304 | tf_op jit(solution)/shard_map/all_to_all | solution.py:400
  100.1 0.0 copy-done.1
  100.1 0.0 copy-done.2
  100.1 0.0 copy-done.3
  100.1 0.0 copy-done.4
  100.1 0.0 copy-done.5
  100.1 4.3 %shard_map.138 = f32[2,32,8192]{2,1,0:T(8,128)} custom-call(f32[4,64,16,128]{3,2,1,0:T(8,128)S(1)} %bitcast.9, bf16[256,256]{1,0:T(8,128)(2,1)S(1)} %copy-done.5, bf16[256,256]{1,0:T(8,128)(2,1)S(1)} %copy-done.4, f32[4,2,128,128]{3,2,1,0:T(8,128)S(1)} %copy-done.3, bf16[4,256,256]{2,1,0:T(8,128)(2,1)S(1)} %copy-done.2, bf16[4,256,256]{2,1,0:T(8,128)(2,1)S(1)} %copy-done.1), custom_call_target="tpu_custom_call" | custom-call | tf_op jit(solution)/shard_map/pallas_call | solution.py:364
Async XLA Ops:
  1.1 13.1 %collective-permute-start.5 = (f32[16,8192]{1,0:T(8,128)S(1)}, f32[16,8192]{1,0:T(8,128)S(1)}, u32[]{:S(2)}, u32[]{:S(2)}) collective-permute-start(f32[16,8192]{1,0:T(8,128)S(1)} %constant_dynamic-slice_fusion), channel_id=1, source_target_pairs={{0,128},{32,160},{64,192},{96,224},{128,0},{160,32},{192,64},{224,... | collective-permute-start | bytes 1572872 | tf_op jit(solution)/shard_map/ppermute | solution.py:387
  3.6 25.0 %copy-start = (f32[32,8192]{1,0:T(8,128)S(1)}, f32[32,8192]{1,0:T(8,128)}, u32[]{:S(2)}) copy-start(f32[32,8192]{1,0:T(8,128)} %taper_own.1) | copy-start | bytes 3145732
  3.6 25.0 %copy-start.6 = (bf16[256,256]{1,0:T(8,128)(2,1)S(1)}, bf16[256,256]{1,0:T(8,128)(2,1)}, u32[]{:S(2)}) copy-start(bf16[256,256]{1,0:T(8,128)(2,1)} %constant.48.clone.wl) | copy-start | bytes 393220
  3.6 25.0 %copy-start.7 = (bf16[256,256]{1,0:T(8,128)(2,1)S(1)}, bf16[256,256]{1,0:T(8,128)(2,1)}, u32[]{:S(2)}) copy-start(bf16[256,256]{1,0:T(8,128)(2,1)} %constant.47.clone.wh) | copy-start | bytes 393220
  3.6 25.0 %copy-start.8 = (f32[2,64,128]{2,1,0:T(8,128)S(1)}, f32[2,64,128]{2,1,0:T(8,128)}, u32[]{:S(2)}) copy-start(f32[2,64,128]{2,1,0:T(8,128)} %constant.46.clone.tw) | copy-start | bytes 196612
  9.9 7.5 %collective-permute-start = (f32[33,8,128]{2,1,0:T(8,128)}, f32[33,8,128]{2,1,0:T(8,128)S(1)}, u32[]{:S(2)}, u32[]{:S(2)}) collective-permute-start(f32[33,8,128]{2,1,0:T(8,128)} %get-tuple-element.17), channel_id=1, source_target_pairs={{0,32},{32,0},{64,96},{96,64},{128,160},{160,128},{192,224},{224,1... | collective-permute-start | bytes 405512 | tf_op jit(solution)/shard_map/ppermute | solution.py:395
  11.3 8.7 %collective-permute-start.1 = (f32[33,8,128]{2,1,0:T(8,128)}, f32[33,8,128]{2,1,0:T(8,128)S(1)}, u32[]{:S(2)}, u32[]{:S(2)}) collective-permute-start(f32[33,8,128]{2,1,0:T(8,128)} %get-tuple-element.18), channel_id=1, source_target_pairs={{0,64},{32,96},{64,0},{96,32},{128,192},{160,224},{192,128},{224,1... | collective-permute-start | bytes 405512 | tf_op jit(solution)/shard_map/ppermute | solution.py:395
  13.9 8.3 %collective-permute-start.2 = (f32[33,8,128]{2,1,0:T(8,128)}, f32[33,8,128]{2,1,0:T(8,128)S(1)}, u32[]{:S(2)}, u32[]{:S(2)}) collective-permute-start(f32[33,8,128]{2,1,0:T(8,128)} %get-tuple-element.19), channel_id=1, source_target_pairs={{0,96},{32,64},{64,32},{96,0},{128,224},{160,192},{192,160},{224,1... | collective-permute-start | bytes 405512 | tf_op jit(solution)/shard_map/ppermute | solution.py:395
  13.9 8.3 %collective-permute-start.3 = (f32[33,8,128]{2,1,0:T(8,128)}, f32[33,8,128]{2,1,0:T(8,128)S(1)}, u32[]{:S(2)}, u32[]{:S(2)}) collective-permute-start(f32[33,8,128]{2,1,0:T(8,128)} %get-tuple-element.20), channel_id=1, source_target_pairs={{0,128},{32,160},{64,192},{96,224},{128,0},{160,32},{192,64},{224,... | collective-permute-start | bytes 405512 | tf_op jit(solution)/shard_map/ppermute | solution.py:395
  14.2 8.0 %collective-permute-start.4 = (f32[33,8,128]{2,1,0:T(8,128)}, f32[33,8,128]{2,1,0:T(8,128)S(1)}, u32[]{:S(2)}, u32[]{:S(2)}) collective-permute-start(f32[33,8,128]{2,1,0:T(8,128)} %get-tuple-element.21), channel_id=1, source_target_pairs={{0,160},{32,128},{64,224},{96,192},{128,32},{160,0},{192,96},{224,... | collective-permute-start | bytes 405512 | tf_op jit(solution)/shard_map/ppermute | solution.py:395
  17.4 8.4 %collective-permute-start.6 = (f32[33,8,128]{2,1,0:T(8,128)}, f32[33,8,128]{2,1,0:T(8,128)S(1)}, u32[]{:S(2)}, u32[]{:S(2)}) collective-permute-start(f32[33,8,128]{2,1,0:T(8,128)} %get-tuple-element.24), channel_id=1, source_target_pairs={{0,192},{32,224},{64,128},{96,160},{128,64},{160,96},{192,0},{224,... | collective-permute-start | bytes 405512 | tf_op jit(solution)/shard_map/ppermute | solution.py:395
  20.0 8.7 %collective-permute-start.7 = (f32[33,8,128]{2,1,0:T(8,128)}, f32[33,8,128]{2,1,0:T(8,128)S(1)}, u32[]{:S(2)}, u32[]{:S(2)}) collective-permute-start(f32[33,8,128]{2,1,0:T(8,128)} %get-tuple-element.25), channel_id=1, source_target_pairs={{0,224},{32,192},{64,160},{96,128},{128,96},{160,64},{192,32},{224... | collective-permute-start | bytes 405512 | tf_op jit(solution)/shard_map/ppermute | solution.py:395
  32.4 67.7 %copy-start.1 = (bf16[4,256,256]{2,1,0:T(8,128)(2,1)S(1)}, bf16[4,256,256]{2,1,0:T(8,128)(2,1)}, u32[]{:S(2)}) copy-start(bf16[4,256,256]{2,1,0:T(8,128)(2,1)} %constant.53.clone.gl) | copy-start | bytes 1572868
  32.4 67.6 %copy-start.2 = (bf16[4,256,256]{2,1,0:T(8,128)(2,1)S(1)}, bf16[4,256,256]{2,1,0:T(8,128)(2,1)}, u32[]{:S(2)}) copy-start(bf16[4,256,256]{2,1,0:T(8,128)(2,1)} %constant.52.clone.gh) | copy-start | bytes 1572868
  32.4 67.6 %copy-start.3 = (f32[4,2,128,128]{3,2,1,0:T(8,128)S(1)}, f32[4,2,128,128]{3,2,1,0:T(8,128)}, u32[]{:S(2)}) copy-start(f32[4,2,128,128]{3,2,1,0:T(8,128)} %constant.51.clone.tw) | copy-start | bytes 1572868
  32.5 67.6 %copy-start.4 = (bf16[256,256]{1,0:T(8,128)(2,1)S(1)}, bf16[256,256]{1,0:T(8,128)(2,1)}, u32[]{:S(2)}) copy-start(bf16[256,256]{1,0:T(8,128)(2,1)} %constant.50.clone.w1l) | copy-start | bytes 393220
  32.5 67.6 %copy-start.5 = (bf16[256,256]{1,0:T(8,128)(2,1)S(1)}, bf16[256,256]{1,0:T(8,128)(2,1)}, u32[]{:S(2)}) copy-start(bf16[256,256]{1,0:T(8,128)(2,1)} %constant.49.clone.w1h) | copy-start | bytes 393220

commit v7 on v6

--- a/solution.py
+++ b/solution.py
@@ -316,7 +316,7 @@
 
     copies = []
     for half in range(2):
-        lax.fori_loop(half * 16, half * 16 + 16, radix, 0, unroll=8)
+        lax.fori_loop(half * 16, half * 16 + 16, radix, 0, unroll=2)
         rows = slice(half * 256, half * 256 + 256)
         for kb in range(4):
             prod = lax.dot_general(gh[kb], bh[kb, rows], NT, preferred_element_type=F32)

time: 105 us -> 105 us (level)
  no operation moved by 1% of the time
where the time goes in v7:
time: 105 us
  blocking collectives  67.6 us (64%)
  Pallas kernels  14.4 us (14%)
  starting transfers between devices  13.3 us (13%)
  waiting for transfers between devices  7.1 us (7%)
  local copies, waits for them, and re-layouts  1.12 us (1%)
    all_to_all x1, blocking collectives, body(): lax.all_to_all(leaving.reshape(256, 16, TILE), ('bl', 'row'), 0, 0, axis_...  67.6 us
    ppermute x7, starting transfers between devices, body(): lax.ppermute(blocks[i], 'bl', [(s, s ^ STEPS[i]) for s in range(N_BL)])  10.7 us
    ppermute x7, waiting for transfers between devices, body(): lax.ppermute(blocks[i], 'bl', [(s, s ^ STEPS[i]) for s in range(N_BL)])  6.84 us
    pallas_call x1, Pallas kernels, grid_call(): pl.pallas_call(grid_kernel, out_shape=[jax.ShapeDtypeStruct((33, 8, TILE)...  6.26 us
    pallas_call x1, Pallas kernels, row_call(): pl.pallas_call(row_kernel, out_shape=jax.ShapeDtypeStruct((2, 32, G), F32...  4.4 us
    pallas_call x1, Pallas kernels, column_call(): pl.pallas_call(column_kernel, out_shape=jax.ShapeDtypeStruct((2, TILE, 16...  3.74 us
    ppermute x1, starting transfers between devices, body(): taper_in = lax.ppermute(given, 'bl', swap)  2.55 us
  transfers between devices with their start and end apart: 8, of which 4 were waited for; matrix products, arithmetic and copies ran while one was open for 1% of the time, Pallas kernels for 6%

profile of v7, /device:TPU:1, one launch (start us, length us, event | category | flops | bytes accessed | tf_op | source)
XLA Modules:
  0.0 104.5 jit_solution(14341284440604477971)
XLA Ops:
  0.0 1.1 %constant_dynamic-slice_fusion = f32[16,8192]{1,0:T(8,128)S(1)} fusion(f32[32,8192]{1,0:T(8,128)} %taper_own.1, s32[]{:T(128)S(6)} %select_n.9), kind=kLoop, calls=%fused_computation.1 | loop fusion | bytes 1048580 | tf_op jit(solution)/shard_map/dynamic_slice | solution.py:386
  1.1 2.6 %collective-permute-start.5 = (f32[16,8192]{1,0:T(8,128)S(1)}, f32[16,8192]{1,0:T(8,128)S(1)}, u32[]{:S(2)}, u32[]{:S(2)}) collective-permute-start(f32[16,8192]{1,0:T(8,128)S(1)} %constant_dynamic-slice_fusion), channel_id=1, source_target_pairs={{0,128},{32,160},{64,192},{96,224},{128,0},{160,32},{192,64},{224,... | collective-permute-start | bytes 1572872 | tf_op jit(solution)/shard_map/ppermute | solution.py:387
  3.6 0.0 copy-start
  3.6 0.0 copy-start.6
  3.6 0.0 copy-start.7
  3.6 0.0 copy-start.8
  3.6 6.3 %shard_map.136 = (f32[33,8,128]{2,1,0:T(8,128)}, f32[33,8,128]{2,1,0:T(8,128)}, f32[33,8,128]{2,1,0:T(8,128)}, f32[33,8,128]{2,1,0:T(8,128)}, f32[33,8,128]{2,1,...) custom-call(s32[1]{0:T(128)} %bitcast.1.me, s32[1,8]{1,0:T(1,128)} %bitcast.14, ...), custom_call_target="tpu_custom_call" | custom-call | flops 4294967296 | bytes 8388608 | tf_op jit(solution)/shard_map/pallas_call | solution.py:163
  9.9 1.4 %collective-permute-start = (f32[33,8,128]{2,1,0:T(8,128)}, f32[33,8,128]{2,1,0:T(8,128)S(1)}, u32[]{:S(2)}, u32[]{:S(2)}) collective-permute-start(f32[33,8,128]{2,1,0:T(8,128)} %get-tuple-element.17), channel_id=1, source_target_pairs={{0,32},{32,0},{64,96},{96,64},{128,160},{160,128},{192,224},{224,1... | collective-permute-start | bytes 405512 | tf_op jit(solution)/shard_map/ppermute | solution.py:395
  11.3 2.6 %collective-permute-start.1 = (f32[33,8,128]{2,1,0:T(8,128)}, f32[33,8,128]{2,1,0:T(8,128)S(1)}, u32[]{:S(2)}, u32[]{:S(2)}) collective-permute-start(f32[33,8,128]{2,1,0:T(8,128)} %get-tuple-element.18), channel_id=1, source_target_pairs={{0,64},{32,96},{64,0},{96,32},{128,192},{160,224},{192,128},{224,1... | collective-permute-start | bytes 405512 | tf_op jit(solution)/shard_map/ppermute | solution.py:395
  13.9 0.0 collective-permute-start.2
  13.9 0.1 collective-permute-start.3
  14.0 0.3 collective-permute-done.5.taper_in
  14.2 3.2 %collective-permute-start.4 = (f32[33,8,128]{2,1,0:T(8,128)}, f32[33,8,128]{2,1,0:T(8,128)S(1)}, u32[]{:S(2)}, u32[]{:S(2)}) collective-permute-start(f32[33,8,128]{2,1,0:T(8,128)} %get-tuple-element.21), channel_id=1, source_target_pairs={{0,160},{32,128},{64,224},{96,192},{128,32},{160,0},{192,96},{224,... | collective-permute-start | bytes 405512 | tf_op jit(solution)/shard_map/ppermute | solution.py:395
  17.4 0.0 collective-permute-done.in1
  17.4 2.5 %collective-permute-start.6 = (f32[33,8,128]{2,1,0:T(8,128)}, f32[33,8,128]{2,1,0:T(8,128)S(1)}, u32[]{:S(2)}, u32[]{:S(2)}) collective-permute-start(f32[33,8,128]{2,1,0:T(8,128)} %get-tuple-element.24), channel_id=1, source_target_pairs={{0,192},{32,224},{64,128},{96,160},{128,64},{160,96},{192,0},{224,... | collective-permute-start | bytes 405512 | tf_op jit(solution)/shard_map/ppermute | solution.py:395
  20.0 0.0 collective-permute-done.1.in2
  20.0 0.9 collective-permute-start.7
  20.9 0.9 broadcast_add_fusion.in0
  21.8 0.4 collective-permute-done.2.in3
  22.2 0.0 collective-permute-done.3.in4
  22.2 0.0 collective-permute-done.4.in5
  22.2 3.6 %collective-permute-done.6.in6 = f32[33,8,128]{2,1,0:T(8,128)S(1)} collective-permute-done((f32[33,8,128]{2,1,0:T(8,128)}, f32[33,8,128]{2,1,0:T(8,128)S(1)}, u32[]{:S(2)}, u32[]{:S(2)}) %collective-permute-start.6) | collective-permute-done | bytes 135200 | tf_op jit(solution)/shard_map/ppermute | solution.py:395
  25.9 2.8 %collective-permute-done.7.in7 = f32[33,8,128]{2,1,0:T(8,128)S(1)} collective-permute-done((f32[33,8,128]{2,1,0:T(8,128)}, f32[33,8,128]{2,1,0:T(8,128)S(1)}, u32[]{:S(2)}, u32[]{:S(2)}) %collective-permute-start.7) | collective-permute-done | bytes 135200 | tf_op jit(solution)/shard_map/ppermute | solution.py:395
  28.7 0.0 copy-done
  28.7 0.0 copy-done.6
  28.7 0.0 copy-done.7
  28.7 0.0 copy-done.8
  28.7 3.7 %shard_map.137 = f32[2,128,16,128]{3,2,1,0:T(8,128)S(1)} custom-call(s32[1]{0:T(128)} %bitcast.side, f32[33,8,128]{2,1,0:T(8,128)S(1)} %broadcast_add_fusion.in0, f32[33,8,128]{2,1,0:T(8,128)S(1)} %collective-permute-done.in1, f32[33,8,128]{2,1,0:T(8,128)S(1)} %collective-permute-done.1.in2, f32[33,8,128]{2,1,0:T(8,128)S(1)} %collective-permute-done.2.in3, ...), custom_call_target="tpu_custom_call" | custom-call | tf_op jit(solution)/shard_map/pallas_call | solution.py:265
  32.4 0.0 copy-start.1
  32.4 0.0 copy-start.2
  32.5 0.0 copy-start.3
  32.5 0.0 copy-start.4
  32.5 0.0 copy-start.5
  32.5 67.6 %all_to_all.5 = f32[256,16,128]{2,1,0:T(8,128)S(1)} all-to-all(f32[256,16,128]{2,1,0:T(8,128)S(1)} %bitcast.10), channel_id=1, replica_groups={{0,64,1,65,2,66,3,67,4,68,5,69,6,70,7,71,8,72,9,73,10,74,11,75,12,76,13..., dimensions={0} | all-to-all | bytes 4194304 | tf_op jit(solution)/shard_map/all_to_all | solution.py:400
  100.1 0.0 copy-done.1
  100.1 0.0 copy-done.2
  100.1 0.0 copy-done.3
  100.1 0.0 copy-done.4
  100.1 0.0 copy-done.5
  100.1 4.4 %shard_map.138 = f32[2,32,8192]{2,1,0:T(8,128)} custom-call(f32[4,64,16,128]{3,2,1,0:T(8,128)S(1)} %bitcast.9, bf16[256,256]{1,0:T(8,128)(2,1)S(1)} %copy-done.5, bf16[256,256]{1,0:T(8,128)(2,1)S(1)} %copy-done.4, f32[4,2,128,128]{3,2,1,0:T(8,128)S(1)} %copy-done.3, bf16[4,256,256]{2,1,0:T(8,128)(2,1)S(1)} %copy-done.2, bf16[4,256,256]{2,1,0:T(8,128)(2,1)S(1)} %copy-done.1), custom_call_target="tpu_custom_call" | custom-call | tf_op jit(solution)/shard_map/pallas_call | solution.py:364
Async XLA Ops:
  1.1 13.1 %collective-permute-start.5 = (f32[16,8192]{1,0:T(8,128)S(1)}, f32[16,8192]{1,0:T(8,128)S(1)}, u32[]{:S(2)}, u32[]{:S(2)}) collective-permute-start(f32[16,8192]{1,0:T(8,128)S(1)} %constant_dynamic-slice_fusion), channel_id=1, source_target_pairs={{0,128},{32,160},{64,192},{96,224},{128,0},{160,32},{192,64},{224,... | collective-permute-start | bytes 1572872 | tf_op jit(solution)/shard_map/ppermute | solution.py:387
  3.6 25.0 %copy-start = (f32[32,8192]{1,0:T(8,128)S(1)}, f32[32,8192]{1,0:T(8,128)}, u32[]{:S(2)}) copy-start(f32[32,8192]{1,0:T(8,128)} %taper_own.1) | copy-start | bytes 3145732
  3.6 25.0 %copy-start.6 = (bf16[256,256]{1,0:T(8,128)(2,1)S(1)}, bf16[256,256]{1,0:T(8,128)(2,1)}, u32[]{:S(2)}) copy-start(bf16[256,256]{1,0:T(8,128)(2,1)} %constant.48.clone.wl) | copy-start | bytes 393220
  3.6 25.0 %copy-start.7 = (bf16[256,256]{1,0:T(8,128)(2,1)S(1)}, bf16[256,256]{1,0:T(8,128)(2,1)}, u32[]{:S(2)}) copy-start(bf16[256,256]{1,0:T(8,128)(2,1)} %constant.47.clone.wh) | copy-start | bytes 393220
  3.6 25.0 %copy-start.8 = (f32[2,64,128]{2,1,0:T(8,128)S(1)}, f32[2,64,128]{2,1,0:T(8,128)}, u32[]{:S(2)}) copy-start(f32[2,64,128]{2,1,0:T(8,128)} %constant.46.clone.tw) | copy-start | bytes 196612
  9.9 7.5 %collective-permute-start = (f32[33,8,128]{2,1,0:T(8,128)}, f32[33,8,128]{2,1,0:T(8,128)S(1)}, u32[]{:S(2)}, u32[]{:S(2)}) collective-permute-start(f32[33,8,128]{2,1,0:T(8,128)} %get-tuple-element.17), channel_id=1, source_target_pairs={{0,32},{32,0},{64,96},{96,64},{128,160},{160,128},{192,224},{224,1... | collective-permute-start | bytes 405512 | tf_op jit(solution)/shard_map/ppermute | solution.py:395
  11.3 8.7 %collective-permute-start.1 = (f32[33,8,128]{2,1,0:T(8,128)}, f32[33,8,128]{2,1,0:T(8,128)S(1)}, u32[]{:S(2)}, u32[]{:S(2)}) collective-permute-start(f32[33,8,128]{2,1,0:T(8,128)} %get-tuple-element.18), channel_id=1, source_target_pairs={{0,64},{32,96},{64,0},{96,32},{128,192},{160,224},{192,128},{224,1... | collective-permute-start | bytes 405512 | tf_op jit(solution)/shard_map/ppermute | solution.py:395
  13.9 8.3 %collective-permute-start.2 = (f32[33,8,128]{2,1,0:T(8,128)}, f32[33,8,128]{2,1,0:T(8,128)S(1)}, u32[]{:S(2)}, u32[]{:S(2)}) collective-permute-start(f32[33,8,128]{2,1,0:T(8,128)} %get-tuple-element.19), channel_id=1, source_target_pairs={{0,96},{32,64},{64,32},{96,0},{128,224},{160,192},{192,160},{224,1... | collective-permute-start | bytes 405512 | tf_op jit(solution)/shard_map/ppermute | solution.py:395
  13.9 8.3 %collective-permute-start.3 = (f32[33,8,128]{2,1,0:T(8,128)}, f32[33,8,128]{2,1,0:T(8,128)S(1)}, u32[]{:S(2)}, u32[]{:S(2)}) collective-permute-start(f32[33,8,128]{2,1,0:T(8,128)} %get-tuple-element.20), channel_id=1, source_target_pairs={{0,128},{32,160},{64,192},{96,224},{128,0},{160,32},{192,64},{224,... | collective-permute-start | bytes 405512 | tf_op jit(solution)/shard_map/ppermute | solution.py:395
  14.2 8.0 %collective-permute-start.4 = (f32[33,8,128]{2,1,0:T(8,128)}, f32[33,8,128]{2,1,0:T(8,128)S(1)}, u32[]{:S(2)}, u32[]{:S(2)}) collective-permute-start(f32[33,8,128]{2,1,0:T(8,128)} %get-tuple-element.21), channel_id=1, source_target_pairs={{0,160},{32,128},{64,224},{96,192},{128,32},{160,0},{192,96},{224,... | collective-permute-start | bytes 405512 | tf_op jit(solution)/shard_map/ppermute | solution.py:395
  17.4 8.4 %collective-permute-start.6 = (f32[33,8,128]{2,1,0:T(8,128)}, f32[33,8,128]{2,1,0:T(8,128)S(1)}, u32[]{:S(2)}, u32[]{:S(2)}) collective-permute-start(f32[33,8,128]{2,1,0:T(8,128)} %get-tuple-element.24), channel_id=1, source_target_pairs={{0,192},{32,224},{64,128},{96,160},{128,64},{160,96},{192,0},{224,... | collective-permute-start | bytes 405512 | tf_op jit(solution)/shard_map/ppermute | solution.py:395
  20.0 8.7 %collective-permute-start.7 = (f32[33,8,128]{2,1,0:T(8,128)}, f32[33,8,128]{2,1,0:T(8,128)S(1)}, u32[]{:S(2)}, u32[]{:S(2)}) collective-permute-start(f32[33,8,128]{2,1,0:T(8,128)} %get-tuple-element.25), channel_id=1, source_target_pairs={{0,224},{32,192},{64,160},{96,128},{128,96},{160,64},{192,32},{224... | collective-permute-start | bytes 405512 | tf_op jit(solution)/shard_map/ppermute | solution.py:395
  32.4 67.6 %copy-start.1 = (bf16[4,256,256]{2,1,0:T(8,128)(2,1)S(1)}, bf16[4,256,256]{2,1,0:T(8,128)(2,1)}, u32[]{:S(2)}) copy-start(bf16[4,256,256]{2,1,0:T(8,128)(2,1)} %constant.53.clone.gl) | copy-start | bytes 1572868
  32.4 67.6 %copy-start.2 = (bf16[4,256,256]{2,1,0:T(8,128)(2,1)S(1)}, bf16[4,256,256]{2,1,0:T(8,128)(2,1)}, u32[]{:S(2)}) copy-start(bf16[4,256,256]{2,1,0:T(8,128)(2,1)} %constant.52.clone.gh) | copy-start | bytes 1572868
  32.5 67.6 %copy-start.3 = (f32[4,2,128,128]{3,2,1,0:T(8,128)S(1)}, f32[4,2,128,128]{3,2,1,0:T(8,128)}, u32[]{:S(2)}) copy-start(f32[4,2,128,128]{3,2,1,0:T(8,128)} %constant.51.clone.tw) | copy-start | bytes 1572868
  32.5 67.6 %copy-start.4 = (bf16[256,256]{1,0:T(8,128)(2,1)S(1)}, bf16[256,256]{1,0:T(8,128)(2,1)}, u32[]{:S(2)}) copy-start(bf16[256,256]{1,0:T(8,128)(2,1)} %constant.50.clone.w1l) | copy-start | bytes 393220
  32.5 67.6 %copy-start.5 = (bf16[256,256]{1,0:T(8,128)(2,1)S(1)}, bf16[256,256]{1,0:T(8,128)(2,1)}, u32[]{:S(2)}) copy-start(bf16[256,256]{1,0:T(8,128)(2,1)} %constant.49.clone.w1h) | copy-start | bytes 393220
